TPU v7x, 32 devices: a whole 2x2x4 slice. The times are simulated.
32 devices in a mesh: dp: 4 (over x, core), ctx: 8 (over z, y).
Axes of the slice: x: 2, y: 2, z: 4, core: 2. Of those that a mesh axis runs over, the one named last changes fastest.
Arguments:
- queries: bfloat16 [4, 1024, 4096], P('dp', 'ctx'), may hold values from -256 to 256
- keys: bfloat16 [4, 1024, 4096], P('dp', 'ctx'), may hold values from -4 to 4
- gate: bfloat16 [4, 1024, 4096], P('dp', 'ctx'), may hold values from -6 to 6
- values: bfloat16 [4, 1024, 4096], P('dp', 'ctx'), may hold values from -6 to 6
- grad_out: bfloat16 [4, 1024, 4096], P('dp', 'ctx'), may hold values from -3 to 3
- doc_start: int32 [4, 1024], P('dp', 'ctx'), may hold values from 0 to 1023, as said below
- filter_taps: float32 [128, 4096], replicated, may hold values from -0.5 to 0.5
Outputs:
- grad_queries: bfloat16 [4, 1024, 4096], P('dp', 'ctx')
- grad_keys: bfloat16 [4, 1024, 4096], P('dp', 'ctx')
- grad_gate: bfloat16 [4, 1024, 4096], P('dp', 'ctx')
- grad_values: bfloat16 [4, 1024, 4096], P('dp', 'ctx')
- grad_filter: float32 [128, 4096], replicated
Inputs may be any that keep to these rules, and one draw needn't show every extreme that they name: `doc_start`: entry t of a sequence is the first position of the document that holds position t: it never exceeds t and never falls along the sequence; every document has at most 640 positions, and every sequence holds one of exactly 640 positions.
All inputs are finite; a program needn't handle non-finite values.
Results may differ from a plain program's by a relative error of at most 0.0087.
Values may be sent and summed in bfloat16 or wider, within the bound.
A program may use at most 192 MiB of HBM per device.

v0:
```python
import jax
import jax.numpy as jnp
from jax import lax
from jax.sharding import PartitionSpec as P

HEADS = 32
ATT_HOPS = 5


lowest_score = -1e30


def passed_along(x, axis, by):
    length = lax.axis_size(axis)
    pairs = [(i, i + by) for i in range(length) if 0 <= i + by < length]
    return lax.ppermute(x, axis, pairs)


def on_device(queries, keys, gate, values, grad_out, doc_start, filter_taps):
    highest = lax.Precision.HIGHEST
    tok_rows = queries.shape[1]
    channel_count = queries.shape[2]
    tap_count = filter_taps.shape[0]
    tap_group = 16
    group_count = tap_count // tap_group
    rim_len = tap_count - 1
    head_width = channel_count // HEADS
    score_scale = head_width ** (-0.5)
    device_rank = lax.axis_index("ctx")
    stream_len = lax.axis_size("ctx") * tok_rows
    own_first = device_rank * tok_rows
    own_pos = own_first + jnp.arange(tok_rows, dtype=jnp.int32)
    own_start = doc_start[0]
    local_values = values[0]
    distance = 1
    first_row = max(0, distance * tok_rows - rim_len)
    behind = [passed_along(local_values[first_row:], "ctx", distance)]
    extended = jnp.concatenate(behind + [local_values], 0).astype(jnp.float32)

    def add_group(group_index, summed):
        base = group_index * tap_group
        block_taps = lax.dynamic_slice_in_dim(filter_taps, base, tap_group, 0)
        region = lax.dynamic_slice_in_dim(
            extended, rim_len - base - (tap_group - 1), tok_rows + tap_group - 1, 0
        )
        for inner in range(tap_group):
            lead = tap_group - 1 - inner
            summed = summed + block_taps[inner][None, :] * region[lead : lead + tok_rows]
        return summed

    mixed = lax.fori_loop(
        0, group_count, add_group, jnp.zeros((tok_rows, channel_count), jnp.float32)
    )
    gate_f32 = gate[0].astype(jnp.float32)
    hyena_out = (gate_f32 * mixed).astype(jnp.bfloat16)
    query_heads = queries[0].reshape(tok_rows, HEADS, head_width)
    key_heads = keys[0].reshape(tok_rows, HEADS, head_width)
    grad_heads = grad_out[0].reshape(tok_rows, HEADS, head_width)
    hyena_heads = hyena_out.reshape(tok_rows, HEADS, head_width)
    grad_f32 = grad_heads.astype(jnp.float32)

    def scores_of(key_piece, offset):
        piece_rows = key_piece.shape[0]
        key_split = key_piece.reshape(piece_rows, HEADS, head_width)
        key_pos = offset + jnp.arange(piece_rows, dtype=jnp.int32)
        allowed = (key_pos[None, :] <= own_pos[:, None]) & (key_pos[None, :] >= own_start[:, None])
        scores = (
            jnp.einsum("ihe,jhe->hij", query_heads, key_split, preferred_element_type=jnp.float32)
            * score_scale
        )
        return (key_split, allowed, scores)

    blocks = [(keys[0], hyena_out, own_first)]
    for distance in range(1, ATT_HOPS + 1):
        key_piece, value_piece = passed_along((keys[0], hyena_out), "ctx", distance)
        blocks.append((key_piece, value_piece, own_first - distance * tok_rows))
    row_top = jnp.full((HEADS, tok_rows), lowest_score, jnp.float32)
    totals = jnp.zeros((HEADS, tok_rows), jnp.float32)
    for key_piece, value_piece, offset in blocks:
        key_split, allowed, scores = scores_of(key_piece, offset)
        new_top = jnp.maximum(row_top, jnp.max(jnp.where(allowed[None], scores, lowest_score), -1))
        weights = jnp.where(allowed[None], jnp.exp(scores - new_top[:, :, None]), 0.0)
        totals = totals * jnp.exp(row_top - new_top) + jnp.sum(weights, -1)
        row_top = new_top
    log_sums = row_top + jnp.log(totals)
    attended = jnp.zeros((tok_rows, HEADS, head_width), jnp.float32)
    for key_piece, value_piece, offset in blocks:
        key_split, allowed, scores = scores_of(key_piece, offset)
        value_split = value_piece.reshape(value_piece.shape[0], HEADS, head_width)
        probs_half = jnp.where(allowed[None], jnp.exp(scores - log_sums[:, :, None]), 0.0).astype(
            jnp.bfloat16
        )
        attended = attended + jnp.einsum(
            "hij,jhe->ihe", probs_half, value_split, preferred_element_type=jnp.float32
        )
    deltas = jnp.einsum("ihe,ihe->hi", grad_f32, attended, precision=highest)
    query_acc = jnp.zeros((tok_rows, HEADS, head_width), jnp.float32)
    for block_index in range(len(blocks)):
        key_piece, value_piece, offset = blocks[block_index]
        key_split, allowed, scores = scores_of(key_piece, offset)
        value_split = value_piece.reshape(value_piece.shape[0], HEADS, head_width)
        probs = jnp.where(allowed[None], jnp.exp(scores - log_sums[:, :, None]), 0.0)
        dprob = jnp.einsum(
            "ihe,jhe->hij", grad_heads, value_split, preferred_element_type=jnp.float32
        )
        dscore = (probs * (dprob - deltas[:, :, None])).astype(jnp.bfloat16)
        query_acc = query_acc + jnp.einsum(
            "hij,jhe->ihe", dscore, key_split, preferred_element_type=jnp.float32
        )
    grad_query = (query_acc * score_scale).reshape(tok_rows, channel_count).astype(jnp.bfloat16)
    own_pos_f32 = own_pos.astype(jnp.float32)
    start_f32 = own_start.astype(jnp.float32)[None, :]

    def query_step(acc_pair, pieces, stats, offset):
        query_piece, grad_piece = pieces
        log_piece, delta_piece, start_piece = stats
        piece_rows = query_piece.shape[0]
        query_piece = query_piece.reshape(piece_rows, HEADS, head_width)
        grad_piece = grad_piece.reshape(piece_rows, HEADS, head_width)
        query_pos = offset + jnp.arange(piece_rows, dtype=jnp.int32)
        start_row = start_piece[0]
        allowed = (own_pos[None, :] <= query_pos[:, None]) & (
            own_pos_f32[None, :] >= start_row[:, None]
        )
        allowed = allowed & (query_pos[:, None] < stream_len)
        scores = (
            jnp.einsum("ihe,jhe->hij", query_piece, key_heads, preferred_element_type=jnp.float32)
            * score_scale
        )
        probs = jnp.where(allowed[None], jnp.exp(scores - log_piece[:, :, None]), 0.0)
        probs_half = probs.astype(jnp.bfloat16)
        dprob = jnp.einsum(
            "ihe,jhe->hij", grad_piece, hyena_heads, preferred_element_type=jnp.float32
        )
        dscore = (probs * (dprob - delta_piece[:, :, None])).astype(jnp.bfloat16)
        acc_dkey, acc_dvalue = acc_pair
        acc_dkey = acc_dkey + jnp.einsum(
            "hij,ihe->jhe", dscore, query_piece, preferred_element_type=jnp.float32
        )
        acc_dvalue = acc_dvalue + jnp.einsum(
            "hij,ihe->jhe", probs_half, grad_piece, preferred_element_type=jnp.float32
        )
        return (acc_dkey, acc_dvalue)

    head_zeros = jnp.zeros((tok_rows, HEADS, head_width), jnp.float32)
    acc_pair = query_step(
        (head_zeros, head_zeros),
        (queries[0], grad_out[0]),
        (log_sums, deltas, start_f32),
        own_first,
    )
    for distance in range(1, ATT_HOPS + 1):
        query_piece, grad_piece = passed_along((queries[0], grad_out[0]), "ctx", -distance)
        stats = passed_along((log_sums, deltas, start_f32), "ctx", -distance)
        acc_pair = query_step(
            acc_pair, (query_piece, grad_piece), stats, own_first + distance * tok_rows
        )
    key_grad = (acc_pair[0] * score_scale).reshape(tok_rows, channel_count)
    value_grad = acc_pair[1].reshape(tok_rows, channel_count)
    grad_key = key_grad.astype(jnp.bfloat16)
    grad_gate = (value_grad * mixed).astype(jnp.bfloat16)
    grad_mixed = (value_grad * gate_f32).astype(jnp.bfloat16)
    distance = 1
    end_row = min(tok_rows, rim_len - (distance - 1) * tok_rows)
    ahead = [passed_along(grad_mixed[:end_row], "ctx", -distance)]
    grad_extended = jnp.concatenate([grad_mixed] + ahead, 0).astype(jnp.float32)

    def back_group(group_index, summed):
        base = group_index * tap_group
        block_taps = lax.dynamic_slice_in_dim(filter_taps, base, tap_group, 0)
        region = lax.dynamic_slice_in_dim(grad_extended, base, tok_rows + tap_group - 1, 0)
        for inner in range(tap_group):
            summed = summed + block_taps[inner][None, :] * region[inner : inner + tok_rows]
        return summed

    grad_values = lax.fori_loop(
        0, group_count, back_group, jnp.zeros((tok_rows, channel_count), jnp.float32)
    )
    grad_local = grad_mixed.astype(jnp.float32)

    def group_sums(group_index):
        base = group_index * tap_group
        region = lax.dynamic_slice_in_dim(
            extended, rim_len - base - (tap_group - 1), tok_rows + tap_group - 1, 0
        )
        rows_out = []
        for inner in range(tap_group):
            lead = tap_group - 1 - inner
            rows_out.append(jnp.sum(grad_local * region[lead : lead + tok_rows], 0))
        return jnp.stack(rows_out, 0)

    filter_terms = lax.map(group_sums, jnp.arange(group_count, dtype=jnp.int32)).reshape(
        tap_count, channel_count
    )
    grad_filter = lax.psum(filter_terms, ("dp", "ctx"))
    return (
        grad_query[None],
        grad_key[None],
        grad_gate[None],
        grad_values.astype(jnp.bfloat16)[None],
        grad_filter,
    )


def solution(mesh):
    placed = (
        P("dp", "ctx", None),
        P("dp", "ctx", None),
        P("dp", "ctx", None),
        P("dp", "ctx", None),
        P("dp", "ctx", None),
        P("dp", "ctx"),
        P(),
    )
    return jax.shard_map(
        on_device,
        mesh=mesh,
        in_specs=placed,
        out_specs=(
            P("dp", "ctx", None),
            P("dp", "ctx", None),
            P("dp", "ctx", None),
            P("dp", "ctx", None),
            P(),
        ),
        check_vma=False,
    )
```

profile of v0, /device:TPU:0, one launch (start us, length us, event | category | flops | bytes accessed | tf_op | source)
XLA Modules:
  0.0 1078.8 jit_solution(17588515615434382356)
XLA Ops:
  15.7 6.5 collective-permute-start.5
  23.5 2.7 select_reduce_fusion.11
  33.2 8.5 collective-permute-start.4
  44.0 3.2 collective-permute-start.2
  47.2 3.2 collective-permute-start.1
  51.2 3.4 collective-permute-start
  54.6 4.0 maximum_convert_fusion
  58.6 172.1 %while.47 = (s32[]{:T(128)}, f32[128,4096]{1,0:T(8,128)}, f32[128,4096]{1,0:T(8,128)}, f32[255,4096]{1,0:T(8,128)}, s32[]{:T(128)}, /*index=5*/s32[]{:T(128)}, s...) while((s32[]{:T(128)}, f32[128,4096]{1,0:T(8,128)}, ...), condition=%wide.region_13.14_spmd.clone, body=%wide.region_12.13_spmd.clone.sunk | while | flops 17301544 | bytes 38535976 | solution.py:51
  61.0 17.9 %fusion.401 = f32[128,4096]{1,0:T(8,128)} fusion(f32[255,4096]{1,0:T(8,128)} %get-tuple-element.727, s32[]{:T(128)S(6)} %select_n.270, s32[]{:T(128)S(6)} %add.1250, s32[]{:T(128)S(6)} %add.1251, s32[]{:T(128)S(6)} %add.1252, s32[]{:T(128)S(6)} %add.1253, s32[]{:T(128)S(6)} %add.1254, s32[]{:T(128)S(6)} %add.1255, s32[]{:T(128)S(6)} %add.1256, ...), kind=kLoop, calls=%fused_computation.34.clone.1 | loop fusion | flops 17301504 | bytes 38010944 | tf_op jit(solution)/shard_map/while/body/eval_jaxpr/add | solution.py:48
  81.4 18.7 %fusion.401 = f32[128,4096]{1,0:T(8,128)} fusion(f32[255,4096]{1,0:T(8,128)} %get-tuple-element.727, s32[]{:T(128)S(6)} %select_n.270, s32[]{:T(128)S(6)} %add.1250, s32[]{:T(128)S(6)} %add.1251, s32[]{:T(128)S(6)} %add.1252, s32[]{:T(128)S(6)} %add.1253, s32[]{:T(128)S(6)} %add.1254, s32[]{:T(128)S(6)} %add.1255, s32[]{:T(128)S(6)} %add.1256, ...), kind=kLoop, calls=%fused_computation.34.clone.1 | loop fusion | flops 17301504 | bytes 38010944 | tf_op jit(solution)/shard_map/while/body/eval_jaxpr/add | solution.py:48
  102.5 19.0 %fusion.401 = f32[128,4096]{1,0:T(8,128)} fusion(f32[255,4096]{1,0:T(8,128)} %get-tuple-element.727, s32[]{:T(128)S(6)} %select_n.270, s32[]{:T(128)S(6)} %add.1250, s32[]{:T(128)S(6)} %add.1251, s32[]{:T(128)S(6)} %add.1252, s32[]{:T(128)S(6)} %add.1253, s32[]{:T(128)S(6)} %add.1254, s32[]{:T(128)S(6)} %add.1255, s32[]{:T(128)S(6)} %add.1256, ...), kind=kLoop, calls=%fused_computation.34.clone.1 | loop fusion | flops 17301504 | bytes 38010944 | tf_op jit(solution)/shard_map/while/body/eval_jaxpr/add | solution.py:48
  123.9 19.5 %fusion.401 = f32[128,4096]{1,0:T(8,128)} fusion(f32[255,4096]{1,0:T(8,128)} %get-tuple-element.727, s32[]{:T(128)S(6)} %select_n.270, s32[]{:T(128)S(6)} %add.1250, s32[]{:T(128)S(6)} %add.1251, s32[]{:T(128)S(6)} %add.1252, s32[]{:T(128)S(6)} %add.1253, s32[]{:T(128)S(6)} %add.1254, s32[]{:T(128)S(6)} %add.1255, s32[]{:T(128)S(6)} %add.1256, ...), kind=kLoop, calls=%fused_computation.34.clone.1 | loop fusion | flops 17301504 | bytes 38010944 | tf_op jit(solution)/shard_map/while/body/eval_jaxpr/add | solution.py:48
  143.4 2.7 constant_dynamic-slice_fusion.34
  146.2 18.3 %fusion.401 = f32[128,4096]{1,0:T(8,128)} fusion(f32[255,4096]{1,0:T(8,128)} %get-tuple-element.727, s32[]{:T(128)S(6)} %select_n.270, s32[]{:T(128)S(6)} %add.1250, s32[]{:T(128)S(6)} %add.1251, s32[]{:T(128)S(6)} %add.1252, s32[]{:T(128)S(6)} %add.1253, s32[]{:T(128)S(6)} %add.1254, s32[]{:T(128)S(6)} %add.1255, s32[]{:T(128)S(6)} %add.1256, ...), kind=kLoop, calls=%fused_computation.34.clone.1 | loop fusion | flops 17301504 | bytes 38010944 | tf_op jit(solution)/shard_map/while/body/eval_jaxpr/add | solution.py:48
  166.9 18.8 %fusion.401 = f32[128,4096]{1,0:T(8,128)} fusion(f32[255,4096]{1,0:T(8,128)} %get-tuple-element.727, s32[]{:T(128)S(6)} %select_n.270, s32[]{:T(128)S(6)} %add.1250, s32[]{:T(128)S(6)} %add.1251, s32[]{:T(128)S(6)} %add.1252, s32[]{:T(128)S(6)} %add.1253, s32[]{:T(128)S(6)} %add.1254, s32[]{:T(128)S(6)} %add.1255, s32[]{:T(128)S(6)} %add.1256, ...), kind=kLoop, calls=%fused_computation.34.clone.1 | loop fusion | flops 17301504 | bytes 38010944 | tf_op jit(solution)/shard_map/while/body/eval_jaxpr/add | solution.py:48
  188.2 20.2 %fusion.401 = f32[128,4096]{1,0:T(8,128)} fusion(f32[255,4096]{1,0:T(8,128)} %get-tuple-element.727, s32[]{:T(128)S(6)} %select_n.270, s32[]{:T(128)S(6)} %add.1250, s32[]{:T(128)S(6)} %add.1251, s32[]{:T(128)S(6)} %add.1252, s32[]{:T(128)S(6)} %add.1253, s32[]{:T(128)S(6)} %add.1254, s32[]{:T(128)S(6)} %add.1255, s32[]{:T(128)S(6)} %add.1256, ...), kind=kLoop, calls=%fused_computation.34.clone.1 | loop fusion | flops 17301504 | bytes 38010944 | tf_op jit(solution)/shard_map/while/body/eval_jaxpr/add | solution.py:48
  210.6 20.1 %fusion.401 = f32[128,4096]{1,0:T(8,128)} fusion(f32[255,4096]{1,0:T(8,128)} %get-tuple-element.727, s32[]{:T(128)S(6)} %select_n.270, s32[]{:T(128)S(6)} %add.1250, s32[]{:T(128)S(6)} %add.1251, s32[]{:T(128)S(6)} %add.1252, s32[]{:T(128)S(6)} %add.1253, s32[]{:T(128)S(6)} %add.1254, s32[]{:T(128)S(6)} %add.1255, s32[]{:T(128)S(6)} %add.1256, ...), kind=kLoop, calls=%fused_computation.34.clone.1 | loop fusion | flops 17301504 | bytes 38010944 | tf_op jit(solution)/shard_map/while/body/eval_jaxpr/add | solution.py:48
  249.4 68.5 %collective-permute-done.22 = bf16[128,4096]{0,1:T(8,128)(2,1)S(1)} collective-permute-done((bf16[128,4096]{0,1:T(8,128)(2,1)}, bf16[128,4096]{0,1:T(8,128)(2,1)S(1)}, u32[]{:S(2)}, u32[]{:S(2)}) %collective-permute-start.22) | collective-permute-done | bytes 1048608 | tf_op jit(solution)/shard_map/ppermute | solution.py:16
  322.3 15.2 %collective-permute-done.17 = bf16[128,4096]{0,1:T(8,128)(2,1)S(1)} collective-permute-done((bf16[128,4096]{0,1:T(8,128)(2,1)S(1)}, bf16[128,4096]{0,1:T(8,128)(2,1)S(1)}, u32[]{:S(2)}, u32[]{:S(2)}) %collective-permute-start.17) | collective-permute-done | bytes 1048608 | tf_op jit(solution)/shard_map/ppermute | solution.py:16
  344.8 6.6 collective-permute-done.24
  352.6 193.9 %collective-permute-done.27 = bf16[128,4096]{0,1:T(8,128)(2,1)S(1)} collective-permute-done((bf16[128,4096]{0,1:T(8,128)(2,1)S(1)}, bf16[128,4096]{0,1:T(8,128)(2,1)S(1)}, u32[]{:S(2)}, u32[]{:S(2)}) %collective-permute-start.27) | collective-permute-done | bytes 1048608 | tf_op jit(solution)/shard_map/ppermute | solution.py:16
  564.9 4.5 collective-permute-done.29
  576.6 2.9 fusion.88
  588.1 2.9 copy.128
  591.0 5.4 fusion.332
  598.6 2.8 collective-permute-start.7
  601.4 7.4 collective-permute-start.8
  613.0 187.7 %while.46 = (s32[]{:T(128)}, f32[8,16,4096]{2,1,0:T(8,128)}, s32[8]{0:T(128)}, f32[255,4096]{1,0:T(8,128)}, f32[128,4096]{1,0:T(8,128)}, /*index=5*/s32[]{:T(128...) while((s32[]{:T(128)}, f32[8,16,4096]{2,1,0:T(8,128)}, ...), condition=%wide.region_33.34_spmd, body=%wide.region_16.33_spmd.sunk | while | flops 16711702 | bytes 36963352 | solution.py:192
  614.9 19.4 %fusion.400 = (f32[4096]{0:T(1024)S(1)}, f32[4096]{0:T(1024)S(1)}, f32[4096]{0:T(1024)S(1)}, f32[4096]{0:T(1024)S(1)}, f32[4096]{0:T(1024)S(1)}, /*index=5*/f32[...) fusion(f32[128,4096]{1,0:T(8,128)} %get-tuple-element.875, ...), kind=kLoop, calls=%fused_computation.1.clone.1 | loop fusion | flops 16711680 | bytes 35913792 | tf_op jit(solution)/shard_map/while/body/eval_jaxpr/reduce_sum | solution.py:189
  638.2 19.5 %fusion.400 = (f32[4096]{0:T(1024)S(1)}, f32[4096]{0:T(1024)S(1)}, f32[4096]{0:T(1024)S(1)}, f32[4096]{0:T(1024)S(1)}, f32[4096]{0:T(1024)S(1)}, /*index=5*/f32[...) fusion(f32[128,4096]{1,0:T(8,128)} %get-tuple-element.875, ...), kind=kLoop, calls=%fused_computation.1.clone.1 | loop fusion | flops 16711680 | bytes 35913792 | tf_op jit(solution)/shard_map/while/body/eval_jaxpr/reduce_sum | solution.py:189
  661.5 20.3 %fusion.400 = (f32[4096]{0:T(1024)S(1)}, f32[4096]{0:T(1024)S(1)}, f32[4096]{0:T(1024)S(1)}, f32[4096]{0:T(1024)S(1)}, f32[4096]{0:T(1024)S(1)}, /*index=5*/f32[...) fusion(f32[128,4096]{1,0:T(8,128)} %get-tuple-element.875, ...), kind=kLoop, calls=%fused_computation.1.clone.1 | loop fusion | flops 16711680 | bytes 35913792 | tf_op jit(solution)/shard_map/while/body/eval_jaxpr/reduce_sum | solution.py:189
  685.7 19.7 %fusion.400 = (f32[4096]{0:T(1024)S(1)}, f32[4096]{0:T(1024)S(1)}, f32[4096]{0:T(1024)S(1)}, f32[4096]{0:T(1024)S(1)}, f32[4096]{0:T(1024)S(1)}, /*index=5*/f32[...) fusion(f32[128,4096]{1,0:T(8,128)} %get-tuple-element.875, ...), kind=kLoop, calls=%fused_computation.1.clone.1 | loop fusion | flops 16711680 | bytes 35913792 | tf_op jit(solution)/shard_map/while/body/eval_jaxpr/reduce_sum | solution.py:189
  709.2 18.8 %fusion.400 = (f32[4096]{0:T(1024)S(1)}, f32[4096]{0:T(1024)S(1)}, f32[4096]{0:T(1024)S(1)}, f32[4096]{0:T(1024)S(1)}, f32[4096]{0:T(1024)S(1)}, /*index=5*/f32[...) fusion(f32[128,4096]{1,0:T(8,128)} %get-tuple-element.875, ...), kind=kLoop, calls=%fused_computation.1.clone.1 | loop fusion | flops 16711680 | bytes 35913792 | tf_op jit(solution)/shard_map/while/body/eval_jaxpr/reduce_sum | solution.py:189
  731.9 19.1 %fusion.400 = (f32[4096]{0:T(1024)S(1)}, f32[4096]{0:T(1024)S(1)}, f32[4096]{0:T(1024)S(1)}, f32[4096]{0:T(1024)S(1)}, f32[4096]{0:T(1024)S(1)}, /*index=5*/f32[...) fusion(f32[128,4096]{1,0:T(8,128)} %get-tuple-element.875, ...), kind=kLoop, calls=%fused_computation.1.clone.1 | loop fusion | flops 16711680 | bytes 35913792 | tf_op jit(solution)/shard_map/while/body/eval_jaxpr/reduce_sum | solution.py:189
  754.8 20.5 %fusion.400 = (f32[4096]{0:T(1024)S(1)}, f32[4096]{0:T(1024)S(1)}, f32[4096]{0:T(1024)S(1)}, f32[4096]{0:T(1024)S(1)}, f32[4096]{0:T(1024)S(1)}, /*index=5*/f32[...) fusion(f32[128,4096]{1,0:T(8,128)} %get-tuple-element.875, ...), kind=kLoop, calls=%fused_computation.1.clone.1 | loop fusion | flops 16711680 | bytes 35913792 | tf_op jit(solution)/shard_map/while/body/eval_jaxpr/reduce_sum | solution.py:189
  779.2 19.6 %fusion.400 = (f32[4096]{0:T(1024)S(1)}, f32[4096]{0:T(1024)S(1)}, f32[4096]{0:T(1024)S(1)}, f32[4096]{0:T(1024)S(1)}, f32[4096]{0:T(1024)S(1)}, /*index=5*/f32[...) fusion(f32[128,4096]{1,0:T(8,128)} %get-tuple-element.875, ...), kind=kLoop, calls=%fused_computation.1.clone.1 | loop fusion | flops 16711680 | bytes 35913792 | tf_op jit(solution)/shard_map/while/body/eval_jaxpr/reduce_sum | solution.py:189
  800.8 3.1 fusion.139
  803.9 3.3 fusion.106
  809.6 4.1 maximum_convert_fusion.1
  813.6 163.7 %while.48 = (s32[]{:T(128)}, f32[128,4096]{1,0:T(8,128)S(1)}, f32[128,4096]{1,0:T(8,128)}, f32[255,4096]{1,0:T(8,128)}, s32[]{:T(128)}, /*index=5*/s32[]{:T(128)...) while((s32[]{:T(128)}, f32[128,4096]{1,0:T(8,128)S(1)}, ...), condition=%wide.region_15.16_spmd.clone, body=%wide.region_14.15_spmd.clone.sunk | while | flops 17301544 | bytes 38535948 | solution.py:176
  816.0 19.1 %fusion.402 = f32[128,4096]{1,0:T(8,128)S(1)} fusion(f32[255,4096]{1,0:T(8,128)} %get-tuple-element.800, s32[]{:T(128)S(6)} %add.1299, s32[]{:T(128)S(6)} %add.1300, s32[]{:T(128)S(6)} %add.1301, s32[]{:T(128)S(6)} %add.1302, s32[]{:T(128)S(6)} %add.1303, s32[]{:T(128)S(6)} %add.1304, s32[]{:T(128)S(6)} %add.1305, s32[]{:T(128)S(6)} %add.1306, ...), kind=kLoop, calls=%fused_computation.82.clone.1 | loop fusion | flops 17301504 | bytes 38010944 | tf_op jit(solution)/shard_map/while/body/eval_jaxpr/add | solution.py:173
  837.6 19.2 %fusion.402 = f32[128,4096]{1,0:T(8,128)S(1)} fusion(f32[255,4096]{1,0:T(8,128)} %get-tuple-element.800, s32[]{:T(128)S(6)} %add.1299, s32[]{:T(128)S(6)} %add.1300, s32[]{:T(128)S(6)} %add.1301, s32[]{:T(128)S(6)} %add.1302, s32[]{:T(128)S(6)} %add.1303, s32[]{:T(128)S(6)} %add.1304, s32[]{:T(128)S(6)} %add.1305, s32[]{:T(128)S(6)} %add.1306, ...), kind=kLoop, calls=%fused_computation.82.clone.1 | loop fusion | flops 17301504 | bytes 38010944 | tf_op jit(solution)/shard_map/while/body/eval_jaxpr/add | solution.py:173
  859.1 17.7 %fusion.402 = f32[128,4096]{1,0:T(8,128)S(1)} fusion(f32[255,4096]{1,0:T(8,128)} %get-tuple-element.800, s32[]{:T(128)S(6)} %add.1299, s32[]{:T(128)S(6)} %add.1300, s32[]{:T(128)S(6)} %add.1301, s32[]{:T(128)S(6)} %add.1302, s32[]{:T(128)S(6)} %add.1303, s32[]{:T(128)S(6)} %add.1304, s32[]{:T(128)S(6)} %add.1305, s32[]{:T(128)S(6)} %add.1306, ...), kind=kLoop, calls=%fused_computation.82.clone.1 | loop fusion | flops 17301504 | bytes 38010944 | tf_op jit(solution)/shard_map/while/body/eval_jaxpr/add | solution.py:173
  879.3 17.1 %fusion.402 = f32[128,4096]{1,0:T(8,128)S(1)} fusion(f32[255,4096]{1,0:T(8,128)} %get-tuple-element.800, s32[]{:T(128)S(6)} %add.1299, s32[]{:T(128)S(6)} %add.1300, s32[]{:T(128)S(6)} %add.1301, s32[]{:T(128)S(6)} %add.1302, s32[]{:T(128)S(6)} %add.1303, s32[]{:T(128)S(6)} %add.1304, s32[]{:T(128)S(6)} %add.1305, s32[]{:T(128)S(6)} %add.1306, ...), kind=kLoop, calls=%fused_computation.82.clone.1 | loop fusion | flops 17301504 | bytes 38010944 | tf_op jit(solution)/shard_map/while/body/eval_jaxpr/add | solution.py:173
  896.4 2.7 constant_dynamic-slice_fusion.35
  899.2 18.4 %fusion.402 = f32[128,4096]{1,0:T(8,128)S(1)} fusion(f32[255,4096]{1,0:T(8,128)} %get-tuple-element.800, s32[]{:T(128)S(6)} %add.1299, s32[]{:T(128)S(6)} %add.1300, s32[]{:T(128)S(6)} %add.1301, s32[]{:T(128)S(6)} %add.1302, s32[]{:T(128)S(6)} %add.1303, s32[]{:T(128)S(6)} %add.1304, s32[]{:T(128)S(6)} %add.1305, s32[]{:T(128)S(6)} %add.1306, ...), kind=kLoop, calls=%fused_computation.82.clone.1 | loop fusion | flops 17301504 | bytes 38010944 | tf_op jit(solution)/shard_map/while/body/eval_jaxpr/add | solution.py:173
  920.1 17.8 %fusion.402 = f32[128,4096]{1,0:T(8,128)S(1)} fusion(f32[255,4096]{1,0:T(8,128)} %get-tuple-element.800, s32[]{:T(128)S(6)} %add.1299, s32[]{:T(128)S(6)} %add.1300, s32[]{:T(128)S(6)} %add.1301, s32[]{:T(128)S(6)} %add.1302, s32[]{:T(128)S(6)} %add.1303, s32[]{:T(128)S(6)} %add.1304, s32[]{:T(128)S(6)} %add.1305, s32[]{:T(128)S(6)} %add.1306, ...), kind=kLoop, calls=%fused_computation.82.clone.1 | loop fusion | flops 17301504 | bytes 38010944 | tf_op jit(solution)/shard_map/while/body/eval_jaxpr/add | solution.py:173
  940.3 17.6 %fusion.402 = f32[128,4096]{1,0:T(8,128)S(1)} fusion(f32[255,4096]{1,0:T(8,128)} %get-tuple-element.800, s32[]{:T(128)S(6)} %add.1299, s32[]{:T(128)S(6)} %add.1300, s32[]{:T(128)S(6)} %add.1301, s32[]{:T(128)S(6)} %add.1302, s32[]{:T(128)S(6)} %add.1303, s32[]{:T(128)S(6)} %add.1304, s32[]{:T(128)S(6)} %add.1305, s32[]{:T(128)S(6)} %add.1306, ...), kind=kLoop, calls=%fused_computation.82.clone.1 | loop fusion | flops 17301504 | bytes 38010944 | tf_op jit(solution)/shard_map/while/body/eval_jaxpr/add | solution.py:173
  960.2 17.2 %fusion.402 = f32[128,4096]{1,0:T(8,128)S(1)} fusion(f32[255,4096]{1,0:T(8,128)} %get-tuple-element.800, s32[]{:T(128)S(6)} %add.1299, s32[]{:T(128)S(6)} %add.1300, s32[]{:T(128)S(6)} %add.1301, s32[]{:T(128)S(6)} %add.1302, s32[]{:T(128)S(6)} %add.1303, s32[]{:T(128)S(6)} %add.1304, s32[]{:T(128)S(6)} %add.1305, s32[]{:T(128)S(6)} %add.1306, ...), kind=kLoop, calls=%fused_computation.82.clone.1 | loop fusion | flops 17301504 | bytes 38010944 | tf_op jit(solution)/shard_map/while/body/eval_jaxpr/add | solution.py:173
  988.2 3.6 add_bitcast_fusion
  991.8 3.1 copy.148
  994.9 2.6 multiply_reduce_fusion
  1004.6 4.0 fusion.109
  1011.0 4.7 fusion.72
  1015.7 4.9 fusion.73
  1020.6 4.0 fusion.74
  1024.6 4.8 fusion.75
  1029.4 7.1 multiply_convert_fusion.1
  1039.2 4.6 fusion.77
  1043.8 5.4 fusion.78
  1049.3 4.3 fusion.79
  1053.7 5.4 fusion.80
  1059.1 7.1 multiply_convert_fusion
  1068.4 3.1 copy.306
  (323 shorter events, 177.5 us)
Async XLA Ops:
  7.2 15.1 %copy-start.42 = (bf16[1,128,4096]{2,1,0:T(8,128)(2,1)S(1)}, bf16[1,128,4096]{2,1,0:T(8,128)(2,1)}, u32[]{:S(2)}) copy-start(bf16[1,128,4096]{2,1,0:T(8,128)(2,1)} %param.13) | copy-start | bytes 3145732
  7.2 1061.2 %all-reduce.2.cloned.1.call-start = ((), (), s32[]{:S(2)}) async-start(), calls=%async_computation | async-start | bytes 4194304 | tf_op jit(solution)/shard_map/psum | solution.py:195
  8.0 15.0 %copy-start.36 = (bf16[1,128,4096]{2,1,0:T(8,128)(2,1)S(1)}, bf16[1,128,4096]{2,1,0:T(8,128)(2,1)}, u32[]{:S(2)}) copy-start(bf16[1,128,4096]{2,1,0:T(8,128)(2,1)} %param.14) | copy-start | bytes 3145732
  8.0 19.5 %collective-permute-start.11 = (f32[1,128]{1,0:T(1,128)S(1)}, f32[1,128]{1,0:T(1,128)S(1)}, u32[]{:S(2)}, u32[]{:S(2)}) collective-permute-start(f32[1,128]{1,0:T(1,128)S(1)} %get-tuple-element.468), channel_id=1, source_target_pairs={{1,0},{2,1},{3,2},{4,3},{5,4},{6,5},{7,6},{9,8},{10,9},{11,10},{12... | collective-permute-start | bytes 1544 | tf_op jit(solution)/shard_map/ppermute | solution.py:16
  9.4 23.8 %collective-permute-start.16 = (f32[1,128]{1,0:T(1,128)S(1)}, f32[1,128]{1,0:T(1,128)S(1)}, u32[]{:S(2)}, u32[]{:S(2)}) collective-permute-start(f32[1,128]{1,0:T(1,128)S(1)} %get-tuple-element.468), channel_id=1, source_target_pairs={{2,0},{3,1},{4,2},{5,3},{6,4},{7,5},{10,8},{11,9},{12,10},{13,11},... | collective-permute-start | bytes 1544 | tf_op jit(solution)/shard_map/ppermute | solution.py:16
  10.7 31.0 %collective-permute-start.21 = (f32[1,128]{1,0:T(1,128)S(1)}, f32[1,128]{1,0:T(1,128)S(1)}, u32[]{:S(2)}, u32[]{:S(2)}) collective-permute-start(f32[1,128]{1,0:T(1,128)S(1)} %get-tuple-element.468), channel_id=1, source_target_pairs={{3,0},{4,1},{5,2},{6,3},{7,4},{11,8},{12,9},{13,10},{14,11},{15,12... | collective-permute-start | bytes 1544 | tf_op jit(solution)/shard_map/ppermute | solution.py:16
  12.0 32.0 %collective-permute-start.26 = (f32[1,128]{1,0:T(1,128)S(1)}, f32[1,128]{1,0:T(1,128)S(1)}, u32[]{:S(2)}, u32[]{:S(2)}) collective-permute-start(f32[1,128]{1,0:T(1,128)S(1)} %get-tuple-element.468), channel_id=1, source_target_pairs={{4,0},{5,1},{6,2},{7,3},{12,8},{13,9},{14,10},{15,11},{20,16},{21,... | collective-permute-start | bytes 1544 | tf_op jit(solution)/shard_map/ppermute | solution.py:16
  15.7 35.5 %collective-permute-start.5 = (bf16[127,4096]{1,0:T(8,128)(2,1)}, bf16[127,4096]{1,0:T(8,128)(2,1)}, u32[]{:S(2)}, u32[]{:S(2)}) collective-permute-start(bf16[127,4096]{1,0:T(8,128)(2,1)} %slice_bitcast_fusion), channel_id=1, source_target_pairs={{0,1},{1,2},{2,3},{3,4},{4,5},{5,6},{6,7},{8,9},{9,10},{10,11},{11... | collective-permute-start | bytes 3121160 | tf_op jit(solution)/shard_map/ppermute | solution.py:16
  23.5 223.6 %copy-start.54 = (pred[128,128]{0,1:T(8,128)(4,1)}, pred[128,128]{0,1:T(8,128)(4,1)S(1)}, u32[]{:S(2)}) copy-start(pred[128,128]{0,1:T(8,128)(4,1)S(1)} %get-tuple-element.461) | copy-start | bytes 49156
  23.5 224.1 %copy-start.50 = (pred[128,128]{0,1:T(8,128)(4,1)}, pred[128,128]{0,1:T(8,128)(4,1)S(1)}, u32[]{:S(2)}) copy-start(pred[128,128]{0,1:T(8,128)(4,1)S(1)} %get-tuple-element.466) | copy-start | bytes 49156
  23.5 224.9 %copy-start.48 = (pred[128,128]{0,1:T(8,128)(4,1)}, pred[128,128]{0,1:T(8,128)(4,1)S(1)}, u32[]{:S(2)}) copy-start(pred[128,128]{0,1:T(8,128)(4,1)S(1)} %get-tuple-element.462) | copy-start | bytes 49156
  23.5 225.4 %copy-start.46 = (pred[128,128]{0,1:T(8,128)(4,1)}, pred[128,128]{0,1:T(8,128)(4,1)S(1)}, u32[]{:S(2)}) copy-start(pred[128,128]{0,1:T(8,128)(4,1)S(1)} %get-tuple-element.463) | copy-start | bytes 49156
  23.5 298.3 %copy-start.44 = (pred[128,128]{0,1:T(8,128)(4,1)}, pred[128,128]{0,1:T(8,128)(4,1)S(1)}, u32[]{:S(2)}) copy-start(pred[128,128]{0,1:T(8,128)(4,1)S(1)} %get-tuple-element.464) | copy-start | bytes 49156
  23.5 320.8 %copy-start.52 = (pred[128,128]{0,1:T(8,128)(4,1)}, pred[128,128]{0,1:T(8,128)(4,1)S(1)}, u32[]{:S(2)}) copy-start(pred[128,128]{0,1:T(8,128)(4,1)S(1)} %get-tuple-element.465) | copy-start | bytes 49156
  27.5 19.7 %collective-permute-start.31 = (f32[1,128]{1,0:T(1,128)S(1)}, f32[1,128]{1,0:T(1,128)S(1)}, u32[]{:S(2)}, u32[]{:S(2)}) collective-permute-start(f32[1,128]{1,0:T(1,128)S(1)} %get-tuple-element.468), channel_id=1, source_target_pairs={{5,0},{6,1},{7,2},{13,8},{14,9},{15,10},{21,16},{22,17},{23,18},{2... | collective-permute-start | bytes 1544 | tf_op jit(solution)/shard_map/ppermute | solution.py:16
  33.2 197.6 %collective-permute-start.4 = (bf16[128,4096]{0,1:T(8,128)(2,1)}, bf16[128,4096]{0,1:T(8,128)(2,1)}, u32[]{:S(2)}, u32[]{:S(2)}) collective-permute-start(bf16[128,4096]{0,1:T(8,128)(2,1)} %bitcast.544), channel_id=1, source_target_pairs={{0,5},{1,6},{2,7},{8,13},{9,14},{10,15},{16,21},{17,22},{18,23},{2... | collective-permute-start | bytes 3145736 | tf_op jit(solution)/shard_map/ppermute | solution.py:16
  41.7 192.6 %collective-permute-start.3 = (bf16[128,4096]{0,1:T(8,128)(2,1)}, bf16[128,4096]{0,1:T(8,128)(2,1)}, u32[]{:S(2)}, u32[]{:S(2)}) collective-permute-start(bf16[128,4096]{0,1:T(8,128)(2,1)} %bitcast.545), channel_id=1, source_target_pairs={{0,4},{1,5},{2,6},{3,7},{8,12},{9,13},{10,14},{11,15},{16,20},{17,... | collective-permute-start | bytes 3145736 | tf_op jit(solution)/shard_map/ppermute | solution.py:16
  44.0 193.4 %collective-permute-start.2 = (bf16[128,4096]{0,1:T(8,128)(2,1)}, bf16[128,4096]{0,1:T(8,128)(2,1)}, u32[]{:S(2)}, u32[]{:S(2)}) collective-permute-start(bf16[128,4096]{0,1:T(8,128)(2,1)} %bitcast.546), channel_id=1, source_target_pairs={{0,3},{1,4},{2,5},{3,6},{4,7},{8,11},{9,12},{10,13},{11,14},{12,15... | collective-permute-start | bytes 3145736 | tf_op jit(solution)/shard_map/ppermute | solution.py:16
  47.2 193.4 %collective-permute-start.1 = (bf16[128,4096]{0,1:T(8,128)(2,1)}, bf16[128,4096]{0,1:T(8,128)(2,1)}, u32[]{:S(2)}, u32[]{:S(2)}) collective-permute-start(bf16[128,4096]{0,1:T(8,128)(2,1)} %bitcast.547), channel_id=1, source_target_pairs={{0,2},{1,3},{2,4},{3,5},{4,6},{5,7},{8,10},{9,11},{10,12},{11,13},... | collective-permute-start | bytes 3145736 | tf_op jit(solution)/shard_map/ppermute | solution.py:16
  51.2 525.3 %copy-start.58 = (pred[128,128]{0,1:T(8,128)(4,1)}, pred[128,128]{0,1:T(8,128)(4,1)S(1)}, u32[]{:S(2)}) copy-start(pred[128,128]{0,1:T(8,128)(4,1)S(1)} %get-tuple-element.458) | copy-start | bytes 49156
  51.2 528.3 %copy-start.60 = (pred[128,128]{0,1:T(8,128)(4,1)}, pred[128,128]{0,1:T(8,128)(4,1)S(1)}, u32[]{:S(2)}) copy-start(pred[128,128]{0,1:T(8,128)(4,1)S(1)} %get-tuple-element.457) | copy-start | bytes 49156
  51.2 531.0 %copy-start.56 = (pred[128,128]{0,1:T(8,128)(4,1)}, pred[128,128]{0,1:T(8,128)(4,1)S(1)}, u32[]{:S(2)}) copy-start(pred[128,128]{0,1:T(8,128)(4,1)S(1)} %get-tuple-element.459) | copy-start | bytes 49156
  51.2 192.5 %collective-permute-start = (bf16[128,4096]{0,1:T(8,128)(2,1)}, bf16[128,4096]{0,1:T(8,128)(2,1)}, u32[]{:S(2)}, u32[]{:S(2)}) collective-permute-start(bf16[128,4096]{0,1:T(8,128)(2,1)} %bitcast.548), channel_id=1, source_target_pairs={{0,1},{1,2},{2,3},{3,4},{4,5},{5,6},{6,7},{8,9},{9,10},{10,11},{11... | collective-permute-start | bytes 3145736 | tf_op jit(solution)/shard_map/ppermute | solution.py:16
  230.8 87.2 %collective-permute-start.22 = (bf16[128,4096]{0,1:T(8,128)(2,1)}, bf16[128,4096]{0,1:T(8,128)(2,1)S(1)}, u32[]{:S(2)}, u32[]{:S(2)}) collective-permute-start(bf16[128,4096]{0,1:T(8,128)(2,1)} %bitcast.457), channel_id=1, source_target_pairs={{3,0},{4,1},{5,2},{6,3},{7,4},{11,8},{12,9},{13,10},{14,11},{15,12... | collective-permute-start | bytes 3145736 | tf_op jit(solution)/shard_map/ppermute | solution.py:16
  234.3 110.0 %copy-start.8 = (f32[32,128,128]{1,2,0:T(8,128)}, f32[32,128,128]{1,2,0:T(8,128)S(1)}, u32[]{:S(2)}) copy-start(f32[32,128,128]{1,2,0:T(8,128)S(1)} %get-tuple-element.470) | copy-start | bytes 6291460
  234.3 103.2 %collective-permute-start.17 = (bf16[128,4096]{0,1:T(8,128)(2,1)S(1)}, bf16[128,4096]{0,1:T(8,128)(2,1)S(1)}, u32[]{:S(2)}, u32[]{:S(2)}) collective-permute-start(bf16[128,4096]{0,1:T(8,128)(2,1)S(1)} %bitcast.460), channel_id=1, source_target_pairs={{2,0},{3,1},{4,2},{5,3},{6,4},{7,5},{10,8},{11,9},{12,10},{13,11},... | collective-permute-start | bytes 3145736 | tf_op jit(solution)/shard_map/ppermute | solution.py:16
  237.4 84.4 %copy-start.11 = (f32[32,128,128]{1,2,0:T(8,128)}, f32[32,128,128]{1,2,0:T(8,128)S(1)}, u32[]{:S(2)}) copy-start(f32[32,128,128]{1,2,0:T(8,128)S(1)} %get-tuple-element.472) | copy-start | bytes 6291460
  237.5 113.9 %collective-permute-start.24 = (bf16[128,4096]{1,0:T(8,128)(2,1)}, bf16[128,4096]{1,0:T(8,128)(2,1)S(1)}, u32[]{:S(2)}, u32[]{:S(2)}) collective-permute-start(bf16[128,4096]{1,0:T(8,128)(2,1)} %bitcast.44), channel_id=1, source_target_pairs={{3,0},{4,1},{5,2},{6,3},{7,4},{11,8},{12,9},{13,10},{14,11},{15,12... | collective-permute-start | bytes 3145736 | tf_op jit(solution)/shard_map/ppermute | solution.py:16
  240.6 8.3 copy-start.13
  240.6 317.2 %collective-permute-start.19 = (bf16[128,4096]{1,0:T(8,128)(2,1)}, bf16[128,4096]{1,0:T(8,128)(2,1)}, u32[]{:S(2)}, u32[]{:S(2)}) collective-permute-start(bf16[128,4096]{1,0:T(8,128)(2,1)} %bitcast.44), channel_id=1, source_target_pairs={{2,0},{3,1},{4,2},{5,3},{6,4},{7,5},{10,8},{11,9},{12,10},{13,11},... | collective-permute-start | bytes 3145736 | tf_op jit(solution)/shard_map/ppermute | solution.py:16
  243.7 97.2 %collective-permute-start.12 = (bf16[128,4096]{0,1:T(8,128)(2,1)S(1)}, bf16[128,4096]{0,1:T(8,128)(2,1)S(1)}, u32[]{:S(2)}, u32[]{:S(2)}) collective-permute-start(bf16[128,4096]{0,1:T(8,128)(2,1)S(1)} %bitcast.464), channel_id=1, source_target_pairs={{1,0},{2,1},{3,2},{4,3},{5,4},{6,5},{7,6},{9,8},{10,9},{11,10},{12... | collective-permute-start | bytes 3145736 | tf_op jit(solution)/shard_map/ppermute | solution.py:16
  248.4 71.3 %copy-start.4 = (bf16[16,8,32,128]{3,2,1,0:T(8,128)(2,1)S(1)}, bf16[16,8,32,128]{3,2,1,0:T(8,128)(2,1)}, u32[]{:S(2)}) copy-start(bf16[16,8,32,128]{3,2,1,0:T(8,128)(2,1)} %copy-done.3) | copy-start | bytes 3145732
  318.0 228.6 %collective-permute-start.27 = (bf16[128,4096]{0,1:T(8,128)(2,1)S(1)}, bf16[128,4096]{0,1:T(8,128)(2,1)S(1)}, u32[]{:S(2)}, u32[]{:S(2)}) collective-permute-start(bf16[128,4096]{0,1:T(8,128)(2,1)S(1)} %bitcast.466), channel_id=1, source_target_pairs={{4,0},{5,1},{6,2},{7,3},{12,8},{13,9},{14,10},{15,11},{20,16},{21,... | collective-permute-start | bytes 3145736 | tf_op jit(solution)/shard_map/ppermute | solution.py:16
  337.5 223.9 %collective-permute-start.14 = (bf16[128,4096]{1,0:T(8,128)(2,1)}, bf16[128,4096]{1,0:T(8,128)(2,1)}, u32[]{:S(2)}, u32[]{:S(2)}) collective-permute-start(bf16[128,4096]{1,0:T(8,128)(2,1)} %bitcast.44), channel_id=1, source_target_pairs={{1,0},{2,1},{3,2},{4,3},{5,4},{6,5},{7,6},{9,8},{10,9},{11,10},{12... | collective-permute-start | bytes 3145736 | tf_op jit(solution)/shard_map/ppermute | solution.py:16
  340.9 211.3 %collective-permute-start.32 = (bf16[128,4096]{0,1:T(8,128)(2,1)S(1)}, bf16[128,4096]{0,1:T(8,128)(2,1)S(1)}, u32[]{:S(2)}, u32[]{:S(2)}) collective-permute-start(bf16[128,4096]{0,1:T(8,128)(2,1)S(1)} %bitcast.467), channel_id=1, source_target_pairs={{5,0},{6,1},{7,2},{13,8},{14,9},{15,10},{21,16},{22,17},{23,18},{2... | collective-permute-start | bytes 3145736 | tf_op jit(solution)/shard_map/ppermute | solution.py:16
  351.4 198.7 %copy-start.43 = (bf16[128,4096]{1,0:T(8,128)(2,1)}, bf16[128,4096]{1,0:T(8,128)(2,1)S(1)}, u32[]{:S(2)}) copy-start(bf16[128,4096]{1,0:T(8,128)(2,1)S(1)} %collective-permute-done.24) | copy-start | bytes 3145732
  351.4 218.1 %collective-permute-start.29 = (bf16[128,4096]{1,0:T(8,128)(2,1)}, bf16[128,4096]{1,0:T(8,128)(2,1)}, u32[]{:S(2)}, u32[]{:S(2)}) collective-permute-start(bf16[128,4096]{1,0:T(8,128)(2,1)} %bitcast.44), channel_id=1, source_target_pairs={{4,0},{5,1},{6,2},{7,3},{12,8},{13,9},{14,10},{15,11},{20,16},{21,... | collective-permute-start | bytes 3145736 | tf_op jit(solution)/shard_map/ppermute | solution.py:16
  546.6 26.4 %collective-permute-start.34 = (bf16[128,4096]{1,0:T(8,128)(2,1)}, bf16[128,4096]{1,0:T(8,128)(2,1)}, u32[]{:S(2)}, u32[]{:S(2)}) collective-permute-start(bf16[128,4096]{1,0:T(8,128)(2,1)} %bitcast.44), channel_id=1, source_target_pairs={{5,0},{6,1},{7,2},{13,8},{14,9},{15,10},{21,16},{22,17},{23,18},{2... | collective-permute-start | bytes 3145736 | tf_op jit(solution)/shard_map/ppermute | solution.py:16
  552.2 24.3 %collective-permute-start.23 = (f32[32,128]{1,0:T(8,128)S(1)}, f32[32,128]{1,0:T(8,128)S(1)}, u32[]{:S(2)}, u32[]{:S(2)}) collective-permute-start(f32[32,128]{1,0:T(8,128)S(1)} %log_add_fusion), channel_id=1, source_target_pairs={{3,0},{4,1},{5,2},{6,3},{7,4},{11,8},{12,9},{13,10},{14,11},{15,12... | collective-permute-start | bytes 49160 | tf_op jit(solution)/shard_map/ppermute | solution.py:16
  557.8 21.7 %collective-permute-start.18 = (f32[32,128]{1,0:T(8,128)S(1)}, f32[32,128]{1,0:T(8,128)S(1)}, u32[]{:S(2)}, u32[]{:S(2)}) collective-permute-start(f32[32,128]{1,0:T(8,128)S(1)} %log_add_fusion), channel_id=1, source_target_pairs={{2,0},{3,1},{4,2},{5,3},{6,4},{7,5},{10,8},{11,9},{12,10},{13,11},... | collective-permute-start | bytes 49160 | tf_op jit(solution)/shard_map/ppermute | solution.py:16
  561.4 19.0 %collective-permute-start.13 = (f32[32,128]{1,0:T(8,128)S(1)}, f32[32,128]{1,0:T(8,128)S(1)}, u32[]{:S(2)}, u32[]{:S(2)}) collective-permute-start(f32[32,128]{1,0:T(8,128)S(1)} %log_add_fusion), channel_id=1, source_target_pairs={{1,0},{2,1},{3,2},{4,3},{5,4},{6,5},{7,6},{9,8},{10,9},{11,10},{12... | collective-permute-start | bytes 49160 | tf_op jit(solution)/shard_map/ppermute | solution.py:16
  569.4 12.8 %collective-permute-start.28 = (f32[32,128]{1,0:T(8,128)S(1)}, f32[32,128]{1,0:T(8,128)S(1)}, u32[]{:S(2)}, u32[]{:S(2)}) collective-permute-start(f32[32,128]{1,0:T(8,128)S(1)} %log_add_fusion), channel_id=1, source_target_pairs={{4,0},{5,1},{6,2},{7,3},{12,8},{13,9},{14,10},{15,11},{20,16},{21,... | collective-permute-start | bytes 49160 | tf_op jit(solution)/shard_map/ppermute | solution.py:16
  573.0 11.1 %collective-permute-start.33 = (f32[32,128]{1,0:T(8,128)S(1)}, f32[32,128]{1,0:T(8,128)S(1)}, u32[]{:S(2)}, u32[]{:S(2)}) collective-permute-start(f32[32,128]{1,0:T(8,128)S(1)} %log_add_fusion), channel_id=1, source_target_pairs={{5,0},{6,1},{7,2},{13,8},{14,9},{15,10},{21,16},{22,17},{23,18},{2... | collective-permute-start | bytes 49160 | tf_op jit(solution)/shard_map/ppermute | solution.py:16
  596.3 382.1 %collective-permute-start.6 = (bf16[128,4096]{1,0:T(8,128)(2,1)}, bf16[128,4096]{1,0:T(8,128)(2,1)}, u32[]{:S(2)}, u32[]{:S(2)}) collective-permute-start(bf16[128,4096]{1,0:T(8,128)(2,1)} %get-tuple-element.453), channel_id=1, source_target_pairs={{0,1},{1,2},{2,3},{3,4},{4,5},{5,6},{6,7},{8,9},{9,10},{10,11},{11... | collective-permute-start | bytes 3145736 | tf_op jit(solution)/shard_map/ppermute | solution.py:16
  598.6 382.8 %collective-permute-start.7 = (bf16[128,4096]{1,0:T(8,128)(2,1)}, bf16[128,4096]{1,0:T(8,128)(2,1)}, u32[]{:S(2)}, u32[]{:S(2)}) collective-permute-start(bf16[128,4096]{1,0:T(8,128)(2,1)} %get-tuple-element.453), channel_id=1, source_target_pairs={{0,2},{1,3},{2,4},{3,5},{4,6},{5,7},{8,10},{9,11},{10,12},{11,13},... | collective-permute-start | bytes 3145736 | tf_op jit(solution)/shard_map/ppermute | solution.py:16
  601.4 382.2 %collective-permute-start.8 = (bf16[128,4096]{1,0:T(8,128)(2,1)}, bf16[128,4096]{1,0:T(8,128)(2,1)}, u32[]{:S(2)}, u32[]{:S(2)}) collective-permute-start(bf16[128,4096]{1,0:T(8,128)(2,1)} %get-tuple-element.453), channel_id=1, source_target_pairs={{0,3},{1,4},{2,5},{3,6},{4,7},{8,11},{9,12},{10,13},{11,14},{12,15... | collective-permute-start | bytes 3145736 | tf_op jit(solution)/shard_map/ppermute | solution.py:16
  608.7 377.0 %collective-permute-start.9 = (bf16[128,4096]{1,0:T(8,128)(2,1)}, bf16[128,4096]{1,0:T(8,128)(2,1)}, u32[]{:S(2)}, u32[]{:S(2)}) collective-permute-start(bf16[128,4096]{1,0:T(8,128)(2,1)} %get-tuple-element.453), channel_id=1, source_target_pairs={{0,4},{1,5},{2,6},{3,7},{8,12},{9,13},{10,14},{11,15},{16,20},{17,... | collective-permute-start | bytes 3145736 | tf_op jit(solution)/shard_map/ppermute | solution.py:16
  611.0 196.2 %collective-permute-start.36 = (bf16[127,4096]{1,0:T(8,128)(2,1)}, bf16[127,4096]{1,0:T(8,128)(2,1)}, u32[]{:S(2)}, u32[]{:S(2)}) collective-permute-start(bf16[127,4096]{1,0:T(8,128)(2,1)} %bitcast.346), channel_id=1, source_target_pairs={{1,0},{2,1},{3,2},{4,3},{5,4},{6,5},{7,6},{9,8},{10,9},{11,10},{12... | collective-permute-start | bytes 3121160 | tf_op jit(solution)/shard_map/ppermute | solution.py:16
  807.2 180.7 %collective-permute-start.10 = (bf16[128,4096]{1,0:T(8,128)(2,1)}, bf16[128,4096]{1,0:T(8,128)(2,1)}, u32[]{:S(2)}, u32[]{:S(2)}) collective-permute-start(bf16[128,4096]{1,0:T(8,128)(2,1)} %get-tuple-element.453), channel_id=1, source_target_pairs={{0,5},{1,6},{2,7},{8,13},{9,14},{10,15},{16,21},{17,22},{18,23},{2... | collective-permute-start | bytes 3145736 | tf_op jit(solution)/shard_map/ppermute | solution.py:16
  994.9 9.7 copy-start.2
  994.9 9.7 copy-start.65
  997.6 11.0 %copy-start.5 = (bf16[16,8,32,128]{3,2,1,0:T(8,128)(2,1)S(1)}, bf16[16,8,32,128]{3,2,1,0:T(8,128)(2,1)}, u32[]{:S(2)}) copy-start(bf16[16,8,32,128]{3,2,1,0:T(8,128)(2,1)} %copy-done.3) | copy-start | bytes 3145732
  997.6 11.0 %copy-start.22 = (f32[32,128,128]{2,1,0:T(8,128)S(1)}, f32[32,128,128]{2,1,0:T(8,128)}, u32[]{:S(2)}) copy-start(f32[32,128,128]{2,1,0:T(8,128)} %fusion.139) | copy-start | bytes 6291460
  997.6 41.6 %collective-permute-start.15 = (f32[32,128]{1,0:T(8,128)S(1)}, f32[32,128]{1,0:T(8,128)S(1)}, u32[]{:S(2)}, u32[]{:S(2)}) collective-permute-start(f32[32,128]{1,0:T(8,128)S(1)} %copy.149), channel_id=1, source_target_pairs={{1,0},{2,1},{3,2},{4,3},{5,4},{6,5},{7,6},{9,8},{10,9},{11,10},{12... | collective-permute-start | bytes 49160 | tf_op jit(solution)/shard_map/ppermute | solution.py:16
  999.2 44.6 %collective-permute-start.20 = (f32[32,128]{1,0:T(8,128)S(1)}, f32[32,128]{1,0:T(8,128)S(1)}, u32[]{:S(2)}, u32[]{:S(2)}) collective-permute-start(f32[32,128]{1,0:T(8,128)S(1)} %copy.149), channel_id=1, source_target_pairs={{2,0},{3,1},{4,2},{5,3},{6,4},{7,5},{10,8},{11,9},{12,10},{13,11},... | collective-permute-start | bytes 49160 | tf_op jit(solution)/shard_map/ppermute | solution.py:16
  1000.5 48.8 %collective-permute-start.25 = (f32[32,128]{1,0:T(8,128)S(1)}, f32[32,128]{1,0:T(8,128)S(1)}, u32[]{:S(2)}, u32[]{:S(2)}) collective-permute-start(f32[32,128]{1,0:T(8,128)S(1)} %copy.149), channel_id=1, source_target_pairs={{3,0},{4,1},{5,2},{6,3},{7,4},{11,8},{12,9},{13,10},{14,11},{15,12... | collective-permute-start | bytes 49160 | tf_op jit(solution)/shard_map/ppermute | solution.py:16
  1002.0 51.7 %collective-permute-start.30 = (f32[32,128]{1,0:T(8,128)S(1)}, f32[32,128]{1,0:T(8,128)S(1)}, u32[]{:S(2)}, u32[]{:S(2)}) collective-permute-start(f32[32,128]{1,0:T(8,128)S(1)} %copy.149), channel_id=1, source_target_pairs={{4,0},{5,1},{6,2},{7,3},{12,8},{13,9},{14,10},{15,11},{20,16},{21,... | collective-permute-start | bytes 49160 | tf_op jit(solution)/shard_map/ppermute | solution.py:16
  1003.3 55.7 %collective-permute-start.35 = (f32[32,128]{1,0:T(8,128)S(1)}, f32[32,128]{1,0:T(8,128)S(1)}, u32[]{:S(2)}, u32[]{:S(2)}) collective-permute-start(f32[32,128]{1,0:T(8,128)S(1)} %copy.149), channel_id=1, source_target_pairs={{5,0},{6,1},{7,2},{13,8},{14,9},{15,10},{21,16},{22,17},{23,18},{2... | collective-permute-start | bytes 49160 | tf_op jit(solution)/shard_map/ppermute | solution.py:16
  1029.4 9.7 copy-start.63
  1029.4 9.7 copy-start.75
  1043.8 5.5 copy-start.23
  1043.8 5.5 copy-start.28
  1043.8 5.5 copy-start.59
  1043.8 5.5 copy-start.69
  (54 other events, 155.8 us)
Sparse Core Ops, SparseCore 0:
  800.9 146.5 all-reduce.1
where the time goes:
time: 1090 us; the launch traced here: 1080 us
  other arithmetic  475 us (44%)
  waiting for transfers between devices  289 us (27%)
  matrix products  110 us (10%)
  local copies, waits for them, and re-layouts  104 us (10%)
  starting transfers between devices  78.9 us (7%)
  between operations  15.8 us (1%)
    ppermute x37, waiting for transfers between devices, passed_along(): return lax.ppermute(x, axis, pairs)  289 us
    reduce_sum x8, other arithmetic, group_sums(): rows_out.append(jnp.sum(grad_local * region[lead:lead + tok_rows], 0))  157 us
    add x8, other arithmetic, add_group(): summed = summed + block_taps[inner][None, :] * region[lead:lead + tok_rows]  153 us
    add x8, other arithmetic, back_group(): summed + block_taps[inner][None, :] * region[inner:inner + tok_rows]  144 us
    ppermute x37, starting transfers between devices, passed_along(): return lax.ppermute(x, axis, pairs)  78.8 us
    dot_general x6, matrix products, query_step(): jnp.einsum('hij,ihe->jhe', dscore, query_piece, preferred_element_type=jn...  30.8 us
    dot_general x6, matrix products, on_device(): jnp.einsum('hij,jhe->ihe', dscore, key_split, preferred_element_type=jnp....  27.9 us
  transfers between devices with their start and end apart: 38, of which 5 were waited for; matrix products, arithmetic and copies ran while one was open for 62% of the time, Pallas kernels for 0%

commit v1 on v0

v1 whole, which is shorter than its diff:
```python
import functools

import jax
import jax.numpy as jnp
from jax import lax
from jax.experimental import pallas as pl
from jax.experimental.pallas import tpu as pltpu
from jax.sharding import PartitionSpec as P

HEADS = 32
HEAD_DIM = 128
LONGEST_DOC = 640
LANES = 128
QUERY_ROWS = 256

f32 = jnp.float32
bf16 = jnp.bfloat16
contract_last = (((1,), (1,)), ((), ()))
contract_first = (((0,), (0,)), ((), ()))


def rows_at(start, size):
    return pl.ds(pl.multiple_of(start, LANES), size)


def mix_forward(seq_blocks, values, gate, taps, taken, turned, mixed, hyena):
    blocks = values.shape[0] // LANES

    @pl.loop(0, blocks)
    def _(n):
        piece = values[rows_at(n * LANES, LANES), :].astype(f32)
        taken[pl.ds(n, LANES, stride=blocks), :] = piece.T

    row = lax.broadcasted_iota(jnp.int32, (LANES, LANES), 0)
    col = lax.broadcasted_iota(jnp.int32, (LANES, LANES), 1)
    block_row = lax.broadcasted_iota(jnp.int32, (blocks, LANES), 0)
    first = lax.rem(block_row, seq_blocks) == 0

    def channel(c, carry):
        own = taken[pl.ds(pl.multiple_of(c * blocks, blocks), blocks), :]
        before = jnp.where(first, 0.0, pltpu.roll(own, 1, 0))
        both = jnp.concatenate([own, before], 1).astype(bf16)
        circle = jnp.broadcast_to(taps[pl.ds(c, 1), :], (LANES, LANES))
        circle = pltpu.roll(circle, 0, 1, stride=1, stride_axis=0)
        near = jnp.where(row <= col, circle, 0.0).astype(bf16)
        far = jnp.where(row > col, circle, 0.0).astype(bf16)
        turned[pl.ds(pl.multiple_of(c * blocks, blocks), blocks), :] = jnp.dot(
            both, jnp.concatenate([near, far], 0), preferred_element_type=f32
        )
        return carry

    lax.fori_loop(0, LANES, channel, 0, unroll=4)

    @pl.loop(0, blocks)
    def _(n):
        at = rows_at(n * LANES, LANES)
        piece = turned[pl.ds(n, LANES, stride=blocks), :].T
        mixed[at, :] = piece
        hyena[at, :] = (gate[at, :].astype(f32) * piece).astype(bf16)


def attend(seq_rows, queries, keys, grad_out, starts, hyena, grad_queries, acc_keys, acc_hyena):
    scale = HEAD_DIM ** (-0.5)
    acc_keys[...] = jnp.zeros_like(acc_keys)
    acc_hyena[...] = jnp.zeros_like(acc_hyena)

    def query_block(base, q_first, k_first, width):
        q_at = rows_at(base + q_first, QUERY_ROWS)
        k_at = rows_at(base + k_first, width)
        q = queries[q_at, :]
        g = grad_out[q_at, :]
        k = keys[k_at, :]
        h = hyena[k_at, :]
        key_pos = k_first + lax.broadcasted_iota(jnp.int32, (QUERY_ROWS, width), 1)
        query_pos = q_first + lax.broadcasted_iota(jnp.int32, (QUERY_ROWS, width), 0)
        allowed = (key_pos <= query_pos) & (key_pos >= starts[q_at, :])
        scores = lax.dot_general(q, k, contract_last, preferred_element_type=f32) * scale
        scores = jnp.where(allowed, scores, -1e30)
        weights = jnp.exp(scores - jnp.max(scores, 1, keepdims=True))
        probs = weights * (1.0 / jnp.sum(weights, 1, keepdims=True))
        half = probs.astype(bf16)
        dprob = lax.dot_general(g, h, contract_last, preferred_element_type=f32)
        delta = jnp.sum(half.astype(f32) * dprob, 1, keepdims=True)
        dscore = (probs * (dprob - delta)).astype(bf16)
        grad_queries[q_at, :] = (jnp.dot(dscore, k, preferred_element_type=f32) * scale).astype(bf16)
        acc_keys[k_at, :] += lax.dot_general(dscore, q, contract_first, preferred_element_type=f32)
        acc_hyena[k_at, :] += lax.dot_general(half, g, contract_first, preferred_element_type=f32)

    full = QUERY_ROWS + LONGEST_DOC
    short = min(seq_rows // QUERY_ROWS, -(-LONGEST_DOC // QUERY_ROWS))

    @pl.loop(0, queries.shape[0] // seq_rows)
    def _(b):
        base = b * seq_rows
        for n in range(short):
            query_block(base, n * QUERY_ROWS, 0, (n + 1) * QUERY_ROWS)

        @pl.loop(short, seq_rows // QUERY_ROWS)
        def _(n):
            query_block(base, n * QUERY_ROWS, n * QUERY_ROWS - LONGEST_DOC, full)


def mix_backward(
    seq_blocks, gate, values, back_taps, taken, turned, mixed, acc_keys, acc_hyena,
    grad_keys, grad_gate, grad_values, grad_filter, given,
):
    scale = HEAD_DIM ** (-0.5)
    blocks = gate.shape[0] // LANES
    row = lax.broadcasted_iota(jnp.int32, (LANES, LANES), 0)
    col = lax.broadcasted_iota(jnp.int32, (LANES, LANES), 1)
    flip = jnp.where(row + col == LANES - 1, 1.0, 0.0).astype(bf16)

    @pl.loop(0, blocks)
    def _(n):
        at = rows_at(n * LANES, LANES)
        grad = acc_hyena[at, :]
        grad_keys[at, :] = (acc_keys[at, :] * scale).astype(bf16)
        grad_gate[at, :] = (grad * mixed[at, :]).astype(bf16)
        grad_mixed = (grad * gate[at, :].astype(f32)).astype(bf16).astype(f32)
        given[pl.ds(n, LANES, stride=blocks), :] = grad_mixed.T
        taken[pl.ds(n, LANES, stride=blocks), :] = lax.dot_general(
            values[at, :], flip, contract_first, preferred_element_type=f32
        )

    block_row = lax.broadcasted_iota(jnp.int32, (blocks, LANES), 0)
    first = lax.rem(block_row, seq_blocks) == 0
    last = lax.rem(block_row, seq_blocks) == seq_blocks - 1

    def channel(c, carry):
        at = pl.ds(pl.multiple_of(c * blocks, blocks), blocks)
        grad = given[at, :]
        after = jnp.where(last, 0.0, pltpu.roll(grad, blocks - 1, 0))
        grads = jnp.concatenate([grad, after], 1).astype(bf16)
        circle = jnp.broadcast_to(back_taps[pl.ds(c, 1), :], (LANES, LANES))
        circle = pltpu.roll(circle, 0, 1, stride=1, stride_axis=0)
        near = jnp.where(row >= col, circle, 0.0).astype(bf16)
        far = jnp.where(row < col, circle, 0.0).astype(bf16)
        turned[at, :] = jnp.dot(grads, jnp.concatenate([near, far], 0), preferred_element_type=f32)
        own = taken[at, :]
        before = jnp.where(first, 0.0, pltpu.roll(own, 1, 0))
        both = jnp.concatenate([own, before], 1).astype(bf16)
        pairs = lax.dot_general(both, grad.astype(bf16), contract_first, preferred_element_type=f32)
        by_lag = jnp.where(row + col >= LANES - 1, pairs[:LANES], pairs[LANES:])
        by_lag = pltpu.roll(by_lag, 1, 1, stride=1, stride_axis=0)
        grad_filter[pl.ds(c, 1), :] = jnp.sum(by_lag, 0, keepdims=True)
        return carry

    lax.fori_loop(0, LANES, channel, 0, unroll=4)

    @pl.loop(0, blocks)
    def _(n):
        piece = turned[pl.ds(n, LANES, stride=blocks), :].T
        grad_values[rows_at(n * LANES, LANES), :] = piece.astype(bf16)


def head_kernel(
    seq_rows, queries, keys, gate, values, grad_out, starts, taps, back_taps,
    grad_queries, grad_keys, grad_gate, grad_values, grad_filter,
    taken, given, turned, mixed, hyena, acc_keys, acc_hyena,
):
    seq_blocks = seq_rows // LANES
    mix_forward(seq_blocks, values, gate, taps, taken, turned, mixed, hyena)
    attend(seq_rows, queries, keys, grad_out, starts, hyena, grad_queries, acc_keys, acc_hyena)
    mix_backward(
        seq_blocks, gate, values, back_taps, taken, turned, mixed, acc_keys, acc_hyena,
        grad_keys, grad_gate, grad_values, grad_filter, given,
    )


def head_grads(seq_rows, queries, keys, gate, values, grad_out, starts, taps):
    rows = queries.shape[0]
    half = jax.ShapeDtypeStruct((rows, LANES), bf16)
    taps = taps.T
    back_taps = jnp.roll(taps[:, ::-1], 1, 1)
    vmem = pl.BlockSpec(memory_space=pltpu.VMEM)
    *grads, grad_filter = pl.pallas_call(
        functools.partial(head_kernel, seq_rows),
        out_shape=[half] * 4 + [jax.ShapeDtypeStruct((LANES, LANES), f32)],
        in_specs=[vmem] * 8,
        out_specs=[vmem] * 5,
        scratch_shapes=[pltpu.VMEM((rows, LANES), f32)] * 4
        + [pltpu.VMEM((rows, LANES), bf16)]
        + [pltpu.VMEM((rows, LANES), f32)] * 2,
        compiler_params=pltpu.CompilerParams(vmem_limit_bytes=48 * 2**20),
    )(queries, keys, gate, values, grad_out, starts.reshape(rows, 1), taps, back_taps)
    return grads, grad_filter.T


def on_device(queries, keys, gate, values, grad_out, doc_start, filter_taps, *, axes, parts):
    tok_rows, channels = queries.shape[1:]
    wide = channels // parts
    seq_rows = lax.axis_size("ctx") * tok_rows

    def to_heads(x):
        x = x[0].reshape(tok_rows, parts, wide).transpose(1, 0, 2)
        return lax.all_to_all(x, axes, 0, 0).reshape(-1, wide)

    def to_rows(x):
        x = lax.all_to_all(x.reshape(parts, tok_rows, wide), axes, 0, 0)
        return x.transpose(1, 0, 2).reshape(1, tok_rows, channels)

    starts = lax.all_gather(doc_start[0], axes, tiled=True)
    own_taps = lax.dynamic_slice_in_dim(filter_taps, lax.axis_index(axes) * wide, wide, 1)
    arrived = [to_heads(x) for x in (queries, keys, gate, values, grad_out)]
    heads = []
    for at in range(0, wide, LANES):
        heads.append(head_grads(
            seq_rows, *(x[:, at : at + LANES] for x in arrived), starts, own_taps[:, at : at + LANES]
        ))
    grads = [jnp.concatenate(pieces, 1) for pieces in zip(*(h[0] for h in heads))]
    own_filter = jnp.concatenate([h[1] for h in heads], 1)
    if "dp" not in axes:
        own_filter = lax.psum(own_filter, "dp")
    grad_filter = lax.all_gather(own_filter, axes, axis=1, tiled=True)
    return (*(to_rows(x) for x in grads), grad_filter)


def solution(mesh):
    axes = ("dp", "ctx")
    if HEADS % (mesh.shape["dp"] * mesh.shape["ctx"]):
        axes = ("ctx",)
    parts = 1
    for axis in axes:
        parts *= mesh.shape[axis]
    rows = P("dp", "ctx", None)
    return jax.shard_map(
        functools.partial(on_device, axes=axes, parts=parts),
        mesh=mesh,
        in_specs=(rows, rows, rows, rows, rows, P("dp", "ctx"), P()),
        out_specs=(rows, rows, rows, rows, P()),
        check_vma=False,
    )
```

time: 1090 us -> 429 us (0.39)
  other arithmetic: 475 us -> 0.08 us
  blocking collectives: 0 us -> 140 us
  waiting for transfers between devices: 289 us -> 149 us
  matrix products: 110 us -> 0 us
  local copies, waits for them, and re-layouts: 104 us -> 36.9 us
  Pallas kernels: 0 us -> 60.5 us
  starting transfers between devices: 78.9 us -> 27.1 us
    add x24 -> x0, other arithmetic: 297 us -> none  [the longest x8 153 us: add_group(): summed = summed + block_taps[inner][None, :] * region[lead:lead + tok_rows]]
    ppermute x37 -> x0, waiting for transfers between devices: 289 us -> none  [passed_along(): return lax.ppermute(x, axis, pairs)]
    reduce_sum x14 -> x0, other arithmetic: 160 us -> none  [the longest x8 157 us: group_sums(): rows_out.append(jnp.sum(grad_local * region[lead:lead + tok_rows], 0))]
    all_to_all x0 -> x7, waiting for transfers between devices: none -> 148 us  [the longest x5 98.9 us: to_heads(): return lax.all_to_all(x, axes, 0, 0).reshape(-1, wide)]
    dot_general x36 -> x0, matrix products: 110 us -> none  [the longest x6 30.8 us: query_step(): jnp.einsum('hij,ihe->jhe', dscore, query_piece, preferred_element_type=jn...]
    all_gather x0 -> x1, blocking collectives: none -> 80.5 us  [on_device(): starts = lax.all_gather(doc_start[0], axes, tiled=True)]
    ppermute x37 -> x0, starting transfers between devices: 78.8 us -> none  [passed_along(): return lax.ppermute(x, axis, pairs)]
    pallas_call x0 -> x1, Pallas kernels: none -> 60.5 us  [head_grads(): pl.pallas_call(functools.partial(head_kernel, seq_rows), out_shape=[half]...]
  transfers between devices with their start and end apart: 38 -> 8, of which waited for: 5 -> 6; matrix products, arithmetic and copies ran while one was open for 62% -> 7% of each run, Pallas kernels for 0% -> 0%
where the time goes in v1:
time: 429 us; the launch traced here: 428 us
  waiting for transfers between devices  149 us (35%)
  blocking collectives  140 us (33%)
  Pallas kernels  60.5 us (14%)
  local copies, waits for them, and re-layouts  36.9 us (9%)
  starting transfers between devices  27.1 us (6%)
  between operations  14.2 us (3%)
    all_to_all x5, waiting for transfers between devices, to_heads(): return lax.all_to_all(x, axes, 0, 0).reshape(-1, wide)  98.9 us
    all_gather x1, blocking collectives, on_device(): starts = lax.all_gather(doc_start[0], axes, tiled=True)  80.5 us
    pallas_call x1, Pallas kernels, head_grads(): pl.pallas_call(functools.partial(head_kernel, seq_rows), out_shape=[half]...  60.5 us
    all_to_all x2, blocking collectives, to_rows(): x = lax.all_to_all(x.reshape(parts, tok_rows, wide), axes, 0, 0)  60 us
    all_to_all x2, waiting for transfers between devices, to_rows(): x = lax.all_to_all(x.reshape(parts, tok_rows, wide), axes, 0, 0)  49.1 us
    all_to_all x5, starting transfers between devices, to_heads(): return lax.all_to_all(x, axes, 0, 0).reshape(-1, wide)  20.9 us
    unnamed x13, local copies, waits for them, and re-layouts  10.4 us
    transpose x4, local copies, waits for them, and re-layouts, to_rows(): return x.transpose(1, 0, 2).reshape(1, tok_rows, channels)  9.3 us
  transfers between devices with their start and end apart: 8, of which 6 were waited for; matrix products, arithmetic and copies ran while one was open for 7% of the time, Pallas kernels for 0%

profile of v1, /device:TPU:0, one launch (start us, length us, event | category | flops | bytes accessed | tf_op | source)
XLA Modules:
  0.0 427.9 jit_solution(59311009145531940)
XLA Ops:
  7.2 0.0 copy-start
  7.2 1.6 copy.36
  8.8 1.4 copy.50
  10.2 7.3 %all-to-all-start = ((bf16[32,128,128]{2,1,0:T(8,128)(2,1)}), bf16[32,128,128]{2,1,0:T(8,128)(2,1)S(1)}, u32[]{:S(2)}, u32[]{:S(2)}) async-start(bf16[32,128,128]{2,1,0:T(8,128)(2,1)} %bitcast.61), calls=%async_computation | async-start | bytes 2097152 | tf_op jit(solution)/shard_map/all_to_all | solution.py:196
  17.5 1.4 copy.37
  18.9 1.4 copy.49
  20.3 24.8 %all-to-all-done = bf16[32,128,128]{2,1,0:T(8,128)(2,1)S(1)} async-done(((bf16[32,128,128]{2,1,0:T(8,128)(2,1)}), bf16[32,128,128]{2,1,0:T(8,128)(2,1)S(1)}, u32[]{:S(2)}, u32[]{:S(2)}) %all-to-all-start) | async-done | bytes 1048608 | tf_op jit(solution)/shard_map/all_to_all | solution.py:196
  45.1 3.4 all-to-all-start.1
  48.5 1.4 copy.38
  49.9 1.4 copy.48
  51.3 24.7 %all-to-all-done.1 = bf16[32,128,128]{2,1,0:T(8,128)(2,1)} async-done(((bf16[32,128,128]{2,1,0:T(8,128)(2,1)}), bf16[32,128,128]{2,1,0:T(8,128)(2,1)}, u32[]{:S(2)}, u32[]{:S(2)}) %all-to-all-start.1) | async-done | bytes 1048608 | tf_op jit(solution)/shard_map/all_to_all | solution.py:196
  76.0 3.4 all-to-all-start.2
  79.4 1.4 copy.39
  80.9 1.4 copy.47
  82.2 24.7 %all-to-all-done.2 = bf16[32,128,128]{2,1,0:T(8,128)(2,1)} async-done(((bf16[32,128,128]{2,1,0:T(8,128)(2,1)}), bf16[32,128,128]{2,1,0:T(8,128)(2,1)}, u32[]{:S(2)}, u32[]{:S(2)}) %all-to-all-start.2) | async-done | bytes 1048608 | tf_op jit(solution)/shard_map/all_to_all | solution.py:196
  107.0 3.4 all-to-all-start.3
  110.4 1.4 copy.40
  111.8 0.0 copy-start.2
  111.8 1.4 copy.46
  113.2 24.7 %all-to-all-done.3 = bf16[32,128,128]{2,1,0:T(8,128)(2,1)} async-done(((bf16[32,128,128]{2,1,0:T(8,128)(2,1)}), bf16[32,128,128]{2,1,0:T(8,128)(2,1)}, u32[]{:S(2)}, u32[]{:S(2)}) %all-to-all-start.3) | async-done | bytes 1048608 | tf_op jit(solution)/shard_map/all_to_all | solution.py:196
  137.9 3.4 all-to-all-start.4
  141.3 0.0 copy-done
  141.4 0.1 copy.35
  141.5 0.1 slice.16
  141.6 0.1 slice.14
  141.6 0.0 copy-done.2
  141.7 80.5 %all-gather = s32[1,4096]{1,0:T(1,128)S(1)} all-gather(s32[1,128]{1,0:T(1,128)S(1)} %copy-done.2), channel_id=2, replica_groups=mesh['dp'=4,'ctx'=8] {'dp','ctx'}, dimensions={1}, use_global_device_ids=true | all-gather | bytes 16896 | tf_op jit(solution)/shard_map/all_gather | solution.py:202
  222.1 2.0 copy.29.starts
  224.1 0.1 pad_maximum_fusion.back_taps
  224.2 0.0 all-to-all-done.4
  224.2 60.5 %shard_map.110 = (bf16[4096,128]{1,0:T(8,128)(2,1)S(1)}, bf16[4096,128]{1,0:T(8,128)(2,1)S(1)}, bf16[4096,128]{1,0:T(8,128)(2,1)S(1)}, bf16[4096,128]{1,0:T(8,128)(2,1)}, f32[128,128]{1,0:T(8,128)}) custom-call(bf16[4096,128]{1,0:T(8,128)(2,1)S(1)} %bitcast.47, bf16[4096,128]{1,0:T(8,128)(2,1)} %bitcast.3.keys, bf16[4096,128]{1,0:T(8,128)(2,1)} %bitcast.5.gate, ...), custom_call_target="tpu_custom_call" | custom-call | tf_op jit(solution)/shard_map/pallas_call | solution.py:176
  284.7 0.0 copy-start.1
  284.7 30.0 %all_to_all.45 = bf16[32,128,128]{2,1,0:T(8,128)(2,1)} all-to-all(bf16[32,128,128]{2,1,0:T(8,128)(2,1)S(1)} %bitcast.53), channel_id=1, replica_groups=mesh['dp'=4,'ctx'=8] {'dp','ctx'}, dimensions={0} | all-to-all | bytes 2097152 | tf_op jit(solution)/shard_map/all_to_all | solution.py:199
  314.7 30.0 %all_to_all.46 = bf16[32,128,128]{2,1,0:T(8,128)(2,1)} all-to-all(bf16[32,128,128]{2,1,0:T(8,128)(2,1)S(1)} %bitcast.52), channel_id=1, replica_groups=mesh['dp'=4,'ctx'=8] {'dp','ctx'}, dimensions={0} | all-to-all | bytes 2097152 | tf_op jit(solution)/shard_map/all_to_all | solution.py:199
  344.7 0.0 copy-done.1
  344.7 2.6 all-to-all-start.7
  347.3 0.0 all-gather.3.cloned.1.call-start
  347.4 0.7 all-gather.3.cloned.1.call-update
  348.1 28.2 %all-to-all-done.7 = bf16[32,128,128]{2,1,0:T(8,128)(2,1)S(1)} async-done(((bf16[32,128,128]{2,1,0:T(8,128)(2,1)}), bf16[32,128,128]{2,1,0:T(8,128)(2,1)S(1)}, u32[]{:S(2)}, u32[]{:S(2)}) %all-to-all-start.7) | async-done | bytes 1048608 | tf_op jit(solution)/shard_map/all_to_all | solution.py:199
  376.3 3.6 all-to-all-start.8
  379.9 2.9 copy.31
  382.8 2.3 reshape.61
  385.1 2.9 copy.30
  387.9 2.3 reshape.59
  390.2 1.6 copy.32
  391.9 2.3 reshape.63
  394.2 20.9 %all-to-all-done.8 = bf16[32,128,128]{2,1,0:T(8,128)(2,1)} async-done(((bf16[32,128,128]{2,1,0:T(8,128)(2,1)}), bf16[32,128,128]{2,1,0:T(8,128)(2,1)}, u32[]{:S(2)}, u32[]{:S(2)}) %all-to-all-start.8) | async-done | bytes 1048608 | tf_op jit(solution)/shard_map/all_to_all | solution.py:199
  415.0 1.9 copy.33
  416.9 1.3 reshape.65
  418.2 0.0 all-gather.3.cloned.1.call-done
  418.2 2.9 copy.34
  (1 shorter events, 0.0 us)
Async XLA Ops:
  7.2 134.2 %copy-start = (f32[128,4096]{1,0:T(8,128)S(1)}, f32[128,4096]{1,0:T(8,128)}, u32[]{:S(2)}) copy-start(f32[128,4096]{1,0:T(8,128)} %param.13) | copy-start | bytes 6291460
  10.2 34.9 %all-to-all-start = ((bf16[32,128,128]{2,1,0:T(8,128)(2,1)}), bf16[32,128,128]{2,1,0:T(8,128)(2,1)S(1)}, u32[]{:S(2)}, u32[]{:S(2)}) async-start(bf16[32,128,128]{2,1,0:T(8,128)(2,1)} %bitcast.61), calls=%async_computation | async-start | bytes 2097152 | tf_op jit(solution)/shard_map/all_to_all | solution.py:196
  45.1 31.0 %all-to-all-start.1 = ((bf16[32,128,128]{2,1,0:T(8,128)(2,1)}), bf16[32,128,128]{2,1,0:T(8,128)(2,1)}, u32[]{:S(2)}, u32[]{:S(2)}) async-start(bf16[32,128,128]{2,1,0:T(8,128)(2,1)} %bitcast.58), calls=%async_computation.1 | async-start | bytes 2097152 | tf_op jit(solution)/shard_map/all_to_all | solution.py:196
  76.0 31.0 %all-to-all-start.2 = ((bf16[32,128,128]{2,1,0:T(8,128)(2,1)}), bf16[32,128,128]{2,1,0:T(8,128)(2,1)}, u32[]{:S(2)}, u32[]{:S(2)}) async-start(bf16[32,128,128]{2,1,0:T(8,128)(2,1)} %bitcast.59), calls=%async_computation.2 | async-start | bytes 2097152 | tf_op jit(solution)/shard_map/all_to_all | solution.py:196
  107.0 31.0 %all-to-all-start.3 = ((bf16[32,128,128]{2,1,0:T(8,128)(2,1)}), bf16[32,128,128]{2,1,0:T(8,128)(2,1)}, u32[]{:S(2)}, u32[]{:S(2)}) async-start(bf16[32,128,128]{2,1,0:T(8,128)(2,1)} %bitcast.60), calls=%async_computation.3 | async-start | bytes 2097152 | tf_op jit(solution)/shard_map/all_to_all | solution.py:196
  111.8 29.8 %copy-start.2 = (s32[1,128]{1,0:T(1,128)S(1)}, s32[1,128]{1,0:T(1,128)}, u32[]{:S(2)}) copy-start(s32[1,128]{1,0:T(1,128)} %param.12) | copy-start | bytes 1540
  137.9 86.3 %all-to-all-start.4 = ((bf16[32,128,128]{2,1,0:T(8,128)(2,1)}), bf16[32,128,128]{2,1,0:T(8,128)(2,1)}, u32[]{:S(2)}, u32[]{:S(2)}) async-start(bf16[32,128,128]{2,1,0:T(8,128)(2,1)} %bitcast.54), calls=%async_computation.4 | async-start | bytes 2097152 | tf_op jit(solution)/shard_map/all_to_all | solution.py:196
  284.7 60.0 %copy-start.1 = (bf16[4096,128]{1,0:T(8,128)(2,1)}, bf16[4096,128]{1,0:T(8,128)(2,1)S(1)}, u32[]{:S(2)}) copy-start(bf16[4096,128]{1,0:T(8,128)(2,1)S(1)} %get-tuple-element.12) | copy-start | bytes 3145732
  344.7 31.6 %all-to-all-start.7 = ((bf16[32,128,128]{2,1,0:T(8,128)(2,1)}), bf16[32,128,128]{2,1,0:T(8,128)(2,1)S(1)}, u32[]{:S(2)}, u32[]{:S(2)}) async-start(bf16[32,128,128]{2,1,0:T(8,128)(2,1)} %bitcast.51), calls=%async_computation.7 | async-start | bytes 2097152 | tf_op jit(solution)/shard_map/all_to_all | solution.py:199
  347.3 70.9 %all-gather.3.cloned.1.call-start = ((), (), s32[]{:S(2)}) async-start(), calls=%async_computation.9 | async-start | bytes 2162688 | tf_op jit(solution)/shard_map/all_gather | solution.py:214
  376.3 38.7 %all-to-all-start.8 = ((bf16[32,128,128]{2,1,0:T(8,128)(2,1)}), bf16[32,128,128]{2,1,0:T(8,128)(2,1)}, u32[]{:S(2)}, u32[]{:S(2)}) async-start(bf16[32,128,128]{2,1,0:T(8,128)(2,1)} %bitcast.18), calls=%async_computation.8 | async-start | bytes 2097152 | tf_op jit(solution)/shard_map/all_to_all | solution.py:199
Sparse Core Ops, SparseCore 0:
  351.2 63.8 all-gather.2

commit v2 on v1

--- a/solution.py
+++ b/solution.py
@@ -23,8 +23,9 @@
     return pl.ds(pl.multiple_of(start, LANES), size)
 
 
-def mix_forward(seq_blocks, values, gate, taps, taken, turned, mixed, hyena):
+def mix_forward(seq_blocks, wait_for, values, gate, taps, taken, turned, mixed, hyena):
     blocks = values.shape[0] // LANES
+    wait_for(0)
 
     @pl.loop(0, blocks)
     def _(n):
@@ -50,19 +51,27 @@
         return carry
 
     lax.fori_loop(0, LANES, channel, 0, unroll=4)
+    flip = jnp.where(row + col == LANES - 1, 1.0, 0.0).astype(bf16)
+    wait_for(1)
 
     @pl.loop(0, blocks)
     def _(n):
         at = rows_at(n * LANES, LANES)
+        taken[pl.ds(n, LANES, stride=blocks), :] = lax.dot_general(
+            values[at, :], flip, contract_first, preferred_element_type=f32
+        )
         piece = turned[pl.ds(n, LANES, stride=blocks), :].T
         mixed[at, :] = piece
         hyena[at, :] = (gate[at, :].astype(f32) * piece).astype(bf16)
 
 
-def attend(seq_rows, queries, keys, grad_out, starts, hyena, grad_queries, acc_keys, acc_hyena):
+def attend(
+    seq_rows, turn, finish, queries, keys, grad_out, starts, hyena, grad_queries, acc_keys, acc_hyena
+):
     scale = HEAD_DIM ** (-0.5)
     acc_keys[...] = jnp.zeros_like(acc_keys)
     acc_hyena[...] = jnp.zeros_like(acc_hyena)
+    sequences = queries.shape[0] // seq_rows
 
     def query_block(base, q_first, k_first, width):
         q_at = rows_at(base + q_first, QUERY_ROWS)
@@ -89,8 +98,9 @@
     full = QUERY_ROWS + LONGEST_DOC
     short = min(seq_rows // QUERY_ROWS, -(-LONGEST_DOC // QUERY_ROWS))
 
-    @pl.loop(0, queries.shape[0] // seq_rows)
-    def _(b):
+    @pl.loop(0, sequences)
+    def _(step):
+        b = lax.rem(step + turn, sequences)
         base = b * seq_rows
         for n in range(short):
             query_block(base, n * QUERY_ROWS, 0, (n + 1) * QUERY_ROWS)
@@ -99,29 +109,30 @@
         def _(n):
             query_block(base, n * QUERY_ROWS, n * QUERY_ROWS - LONGEST_DOC, full)
 
-
-def mix_backward(
-    seq_blocks, gate, values, back_taps, taken, turned, mixed, acc_keys, acc_hyena,
-    grad_keys, grad_gate, grad_values, grad_filter, given,
+        finish(b)
+
+
+def finish_sequence(
+    b, seq_blocks, gate, mixed, acc_keys, acc_hyena, grad_keys, grad_gate, given
 ):
     scale = HEAD_DIM ** (-0.5)
     blocks = gate.shape[0] // LANES
-    row = lax.broadcasted_iota(jnp.int32, (LANES, LANES), 0)
-    col = lax.broadcasted_iota(jnp.int32, (LANES, LANES), 1)
-    flip = jnp.where(row + col == LANES - 1, 1.0, 0.0).astype(bf16)
-
-    @pl.loop(0, blocks)
-    def _(n):
+
+    @pl.loop(0, seq_blocks)
+    def _(step):
+        n = b * seq_blocks + step
         at = rows_at(n * LANES, LANES)
         grad = acc_hyena[at, :]
         grad_keys[at, :] = (acc_keys[at, :] * scale).astype(bf16)
         grad_gate[at, :] = (grad * mixed[at, :]).astype(bf16)
         grad_mixed = (grad * gate[at, :].astype(f32)).astype(bf16).astype(f32)
         given[pl.ds(n, LANES, stride=blocks), :] = grad_mixed.T
-        taken[pl.ds(n, LANES, stride=blocks), :] = lax.dot_general(
-            values[at, :], flip, contract_first, preferred_element_type=f32
-        )
-
+
+
+def mix_backward(seq_blocks, back_taps, taken, given, turned, grad_values, by_channel):
+    blocks = given.shape[0] // LANES
+    row = lax.broadcasted_iota(jnp.int32, (LANES, LANES), 0)
+    col = lax.broadcasted_iota(jnp.int32, (LANES, LANES), 1)
     block_row = lax.broadcasted_iota(jnp.int32, (blocks, LANES), 0)
     first = lax.rem(block_row, seq_blocks) == 0
     last = lax.rem(block_row, seq_blocks) == seq_blocks - 1
@@ -142,7 +153,7 @@
         pairs = lax.dot_general(both, grad.astype(bf16), contract_first, preferred_element_type=f32)
         by_lag = jnp.where(row + col >= LANES - 1, pairs[:LANES], pairs[LANES:])
         by_lag = pltpu.roll(by_lag, 1, 1, stride=1, stride_axis=0)
-        grad_filter[pl.ds(c, 1), :] = jnp.sum(by_lag, 0, keepdims=True)
+        by_channel[pl.ds(c, 1), :] = jnp.sum(by_lag, 0, keepdims=True)
         return carry
 
     lax.fori_loop(0, LANES, channel, 0, unroll=4)
@@ -154,65 +165,165 @@
 
 
 def head_kernel(
-    seq_rows, queries, keys, gate, values, grad_out, starts, taps, back_taps,
-    grad_queries, grad_keys, grad_gate, grad_values, grad_filter,
-    taken, given, turned, mixed, hyena, acc_keys, acc_hyena,
+    axes, queries, keys, gate, values, grad_out, starts, taps, back_taps,
+    to_queries, to_keys, to_gate, to_values, to_filter,
+    arrived, starts_in, starts_col, taken, given, turned, mixed, hyena, acc_keys, acc_hyena,
+    grad_queries, grad_keys, grad_gate, grad_values, by_channel, grad_filter,
+    in_sent, in_got, out_sent, out_got,
 ):
+    tok_rows = queries.shape[0]
+    per_seq = lax.axis_size("ctx")
+    parts = per_seq * (lax.axis_size("dp") if "dp" in axes else 1)
+    seq_rows = per_seq * tok_rows
     seq_blocks = seq_rows // LANES
-    mix_forward(seq_blocks, values, gate, taps, taken, turned, mixed, hyena)
-    attend(seq_rows, queries, keys, grad_out, starts, hyena, grad_queries, acc_keys, acc_hyena)
-    mix_backward(
-        seq_blocks, gate, values, back_taps, taken, turned, mixed, acc_keys, acc_hyena,
-        grad_keys, grad_gate, grad_values, grad_filter, given,
+    me, turn = lax.axis_index("ctx"), 0
+    if "dp" in axes:
+        turn = lax.axis_index("dp")
+        me = turn * per_seq + me
+
+    def device(peer):
+        if "dp" in axes:
+            return {"dp": lax.div(peer, per_seq), "ctx": lax.rem(peer, per_seq)}
+        return {"ctx": peer}
+
+    def others(act):
+        @pl.loop(1, parts)
+        def _(step):
+            act(lax.rem(me + step, parts))
+
+    def send(source, target, sent, got, peer):
+        pltpu.make_async_remote_copy(
+            src_ref=source, dst_ref=target, send_sem=sent, recv_sem=got,
+            device_id=device(peer), device_id_type=pl.DeviceIdType.MESH,
+        ).start()
+
+    def lanes_of(part):
+        return pl.ds(pl.multiple_of(part * LANES, LANES), LANES)
+
+    def rows_of(part):
+        return rows_at(part * tok_rows, tok_rows)
+
+    barrier = pltpu.get_barrier_semaphore()
+    others(lambda peer: pl.semaphore_signal(
+        barrier, inc=1, device_id=device(peer), device_id_type=pl.DeviceIdType.MESH
+    ))
+    pl.semaphore_wait(barrier, parts - 1)
+
+    incoming = (values, gate, keys, queries, grad_out)
+    for at, source in enumerate(incoming):
+        landing = arrived.at[at, rows_of(me)]
+        others(lambda peer: send(
+            source.at[:, lanes_of(peer)], landing, in_sent.at[at], in_got.at[at], peer
+        ))
+        pltpu.make_async_copy(source.at[:, lanes_of(me)], landing, in_got.at[at]).start()
+        if at == 1:
+            others(lambda peer: send(starts, starts_in.at[me], in_sent.at[5], in_got.at[5], peer))
+            pltpu.make_async_copy(starts, starts_in.at[me], in_got.at[5]).start()
+
+    def wait_for(at):
+        whole = starts_in if at == 5 else arrived.at[at]
+        pltpu.make_async_copy(whole, whole, in_got.at[at]).wait()
+
+    v, gates, k, q, g = (arrived.at[at] for at in range(5))
+    mix_forward(seq_blocks, wait_for, v, gates, taps, taken, turned, mixed, hyena)
+    wait_for(5)
+
+    @pl.loop(0, parts)
+    def _(part):
+        line = starts_in[part].astype(f32)[:1]
+        turned_line = jnp.broadcast_to(line, (LANES, LANES)).T
+        starts_col[rows_at(part * LANES, LANES), :] = turned_line[:, :1].astype(jnp.int32)
+
+    for at in (2, 3, 4):
+        wait_for(at)
+
+    results = ((grad_queries, to_queries), (grad_keys, to_keys), (grad_gate, to_gate))
+
+    def give(at, source, target, peer):
+        @pl.when(peer != me)
+        def _():
+            send(source, target, out_sent.at[at], out_got.at[at], peer)
+
+        @pl.when(peer == me)
+        def _():
+            pltpu.make_async_copy(source, target, out_got.at[at]).start()
+
+    def finish(b):
+        finish_sequence(
+            b, seq_blocks, gates, mixed, acc_keys, acc_hyena, grad_keys, grad_gate, given
+        )
+        for at, (source, target) in enumerate(results):
+            @pl.loop(0, per_seq)
+            def _(step):
+                peer = b * per_seq + lax.rem(step + lax.axis_index("ctx"), per_seq)
+                give(at, source.at[rows_of(peer)], target.at[:, lanes_of(me)], peer)
+
+    attend(
+        seq_rows, turn, finish, q, k, g, starts_col, hyena, grad_queries, acc_keys, acc_hyena
     )
-
-
-def head_grads(seq_rows, queries, keys, gate, values, grad_out, starts, taps):
-    rows = queries.shape[0]
-    half = jax.ShapeDtypeStruct((rows, LANES), bf16)
-    taps = taps.T
-    back_taps = jnp.roll(taps[:, ::-1], 1, 1)
-    vmem = pl.BlockSpec(memory_space=pltpu.VMEM)
-    *grads, grad_filter = pl.pallas_call(
-        functools.partial(head_kernel, seq_rows),
-        out_shape=[half] * 4 + [jax.ShapeDtypeStruct((LANES, LANES), f32)],
-        in_specs=[vmem] * 8,
-        out_specs=[vmem] * 5,
-        scratch_shapes=[pltpu.VMEM((rows, LANES), f32)] * 4
-        + [pltpu.VMEM((rows, LANES), bf16)]
-        + [pltpu.VMEM((rows, LANES), f32)] * 2,
-        compiler_params=pltpu.CompilerParams(vmem_limit_bytes=48 * 2**20),
-    )(queries, keys, gate, values, grad_out, starts.reshape(rows, 1), taps, back_taps)
-    return grads, grad_filter.T
+    mix_backward(seq_blocks, back_taps, taken, given, turned, grad_values, by_channel)
+    grad_filter[...] = by_channel[...].T.astype(bf16)
+    own_lanes = lanes_of(me)
+    others(lambda peer: send(
+        grad_values.at[rows_of(peer)], to_values.at[:, own_lanes], out_sent.at[3], out_got.at[3], peer
+    ))
+    pltpu.make_async_copy(
+        grad_values.at[rows_of(me)], to_values.at[:, own_lanes], out_got.at[3]
+    ).start()
+    others(lambda peer: send(
+        grad_filter, to_filter.at[:, own_lanes], out_sent.at[4], out_got.at[4], peer
+    ))
+    pltpu.make_async_copy(grad_filter, to_filter.at[:, own_lanes], out_got.at[4]).start()
+
+    remote = pl.ds(0, (parts - 1) * LANES)
+    for at in range(5):
+        sent = incoming[at].at[:, remote]
+        pltpu.make_async_copy(sent, sent, in_sent.at[at]).wait()
+    sent = starts_in.at[pl.ds(0, parts - 1)]
+    pltpu.make_async_copy(sent, sent, in_sent.at[5]).wait()
+    for at, target in enumerate((to_queries, to_keys, to_gate, to_values, to_filter)):
+        pltpu.make_async_copy(target, target, out_got.at[at]).wait()
+        sent = target.at[:, remote]
+        pltpu.make_async_copy(sent, sent, out_sent.at[at]).wait()
 
 
 def on_device(queries, keys, gate, values, grad_out, doc_start, filter_taps, *, axes, parts):
     tok_rows, channels = queries.shape[1:]
-    wide = channels // parts
-    seq_rows = lax.axis_size("ctx") * tok_rows
-
-    def to_heads(x):
-        x = x[0].reshape(tok_rows, parts, wide).transpose(1, 0, 2)
-        return lax.all_to_all(x, axes, 0, 0).reshape(-1, wide)
-
-    def to_rows(x):
-        x = lax.all_to_all(x.reshape(parts, tok_rows, wide), axes, 0, 0)
-        return x.transpose(1, 0, 2).reshape(1, tok_rows, channels)
-
-    starts = lax.all_gather(doc_start[0], axes, tiled=True)
-    own_taps = lax.dynamic_slice_in_dim(filter_taps, lax.axis_index(axes) * wide, wide, 1)
-    arrived = [to_heads(x) for x in (queries, keys, gate, values, grad_out)]
-    heads = []
-    for at in range(0, wide, LANES):
-        heads.append(head_grads(
-            seq_rows, *(x[:, at : at + LANES] for x in arrived), starts, own_taps[:, at : at + LANES]
-        ))
-    grads = [jnp.concatenate(pieces, 1) for pieces in zip(*(h[0] for h in heads))]
-    own_filter = jnp.concatenate([h[1] for h in heads], 1)
+    rows = parts * tok_rows
+    own_taps = lax.dynamic_slice_in_dim(filter_taps, lax.axis_index(axes) * LANES, LANES, 1).T
+    back_taps = jnp.roll(own_taps[:, ::-1], 1, 1)
+    starts = jnp.broadcast_to(doc_start, (8, tok_rows))
+    vmem = pl.BlockSpec(memory_space=pltpu.VMEM)
+    anywhere = pl.BlockSpec(memory_space=pl.ANY)
+    wide = pltpu.VMEM((rows, LANES), f32)
+    narrow = pltpu.VMEM((rows, LANES), bf16)
+    *grads, grad_filter = pl.pallas_call(
+        functools.partial(head_kernel, axes),
+        out_shape=[jax.ShapeDtypeStruct((tok_rows, channels), bf16)] * 4
+        + [jax.ShapeDtypeStruct(filter_taps.shape, bf16)],
+        in_specs=[anywhere] * 5 + [vmem] * 3,
+        out_specs=[anywhere] * 5,
+        scratch_shapes=[
+            pltpu.VMEM((5, rows, LANES), bf16),
+            pltpu.VMEM((parts, 8, tok_rows), jnp.int32),
+            pltpu.VMEM((rows, 1), jnp.int32),
+            wide, wide, wide, wide, narrow, wide, wide,
+            narrow, narrow, narrow, narrow,
+            pltpu.VMEM((LANES, LANES), f32),
+            pltpu.VMEM((LANES, LANES), bf16),
+            pltpu.SemaphoreType.DMA((6,)),
+            pltpu.SemaphoreType.DMA((6,)),
+            pltpu.SemaphoreType.DMA((5,)),
+            pltpu.SemaphoreType.DMA((5,)),
+        ],
+        compiler_params=pltpu.CompilerParams(
+            collective_id=0, has_side_effects=True, vmem_limit_bytes=48 * 2**20
+        ),
+    )(queries[0], keys[0], gate[0], values[0], grad_out[0], starts, own_taps, back_taps)
+    grad_filter = grad_filter.astype(f32)
     if "dp" not in axes:
-        own_filter = lax.psum(own_filter, "dp")
-    grad_filter = lax.all_gather(own_filter, axes, axis=1, tiled=True)
-    return (*(to_rows(x) for x in grads), grad_filter)
+        grad_filter = lax.psum(grad_filter, "dp")
+    return (*(x[None] for x in grads), grad_filter)
 
 
 def solution(mesh):

time: 429 us -> 250 us (0.58)
  Pallas kernels: 60.5 us -> 242 us
  waiting for transfers between devices: 149 us -> 0 us
  blocking collectives: 140 us -> 0 us
  local copies, waits for them, and re-layouts: 36.9 us -> 5.74 us
  starting transfers between devices: 27.1 us -> 0 us
  between operations: 14.2 us -> 0.68 us
    pallas_call x1, Pallas kernels: 60.5 us -> 242 us  [on_device(): pl.pallas_call(functools.partial(head_kernel, axes), out_shape=[jax.Shape...]
    all_to_all x7 -> x0, waiting for transfers between devices: 148 us -> none  [the longest x5 98.9 us: to_heads(): return lax.all_to_all(x, axes, 0, 0).reshape(-1, wide)]
    all_gather x1 -> x0, blocking collectives: 80.5 us -> none  [on_device(): starts = lax.all_gather(doc_start[0], axes, tiled=True)]
    all_to_all x2 -> x0, blocking collectives: 60 us -> none  [to_rows(): x = lax.all_to_all(x.reshape(parts, tok_rows, wide), axes, 0, 0)]
    all_to_all x7 -> x0, starting transfers between devices: 27.1 us -> none  [the longest x5 20.9 us: to_heads(): return lax.all_to_all(x, axes, 0, 0).reshape(-1, wide)]
    reshape x5 -> x0, local copies, waits for them, and re-layouts: 10.1 us -> none  [the longest x4 8.15 us: to_rows(): return x.transpose(1, 0, 2).reshape(1, tok_rows, channels)]
    transpose x4 -> x0, local copies, waits for them, and re-layouts: 9.3 us -> none  [to_rows(): return x.transpose(1, 0, 2).reshape(1, tok_rows, channels)]
    another operation x5 -> x0, local copies, waits for them, and re-layouts: 6.9 us -> none  [to_heads(): x = x[0].reshape(tok_rows, parts, wide).transpose(1, 0, 2)]
  transfers between devices with their start and end apart: 8 -> 0, of which waited for: 6 -> 0; matrix products, arithmetic and copies ran while one was open for 7% -> 0% of each run, Pallas kernels for 0% -> 0%
where the time goes in v2:
time: 250 us
  Pallas kernels  242 us (97%)
  local copies, waits for them, and re-layouts  5.74 us (2%)
    pallas_call x1, Pallas kernels, on_device(): pl.pallas_call(functools.partial(head_kernel, axes), out_shape=[jax.Shape...  242 us

profile of v2, /device:TPU:0, one launch (start us, length us, event | category | flops | bytes accessed | tf_op | source)
XLA Modules:
  0.0 249.7 jit_solution(4216015735394206730)
XLA Ops:
  0.6 0.0 copy-start
  0.7 0.8 broadcast_in_dim.20.starts
  1.5 0.8 copy-done
  2.3 0.1 copy.13
  2.4 0.1 slice.16
  2.4 0.1 slice.14
  2.5 0.1 pad_maximum_fusion.back_taps
  2.6 241.7 %shard_map.110 = (bf16[128,4096]{1,0:T(8,128)(2,1)S(1)}, bf16[128,4096]{1,0:T(8,128)(2,1)S(1)}, bf16[128,4096]{1,0:T(8,128)(2,1)S(1)}, bf16[128,4096]{1,0:T(8,128)(2,1)S(1)}, bf16[128,4096]{1,0:T(8,128)(2,1)S(1)}) custom-call(bf16[128,4096]{1,0:T(8,128)(2,1)} %bitcast.19, bf16[128,4096]{1,0:T(8,128)(2,1)} %bitcast.20, bf16[128,4096]{1,0:T(8,128)(2,1)} %bitcast.21, ...), custom_call_target="tpu_custom_call" | custom-call | tf_op jit(solution)/shard_map/pallas_call | solution.py:300
  244.3 1.5 convert_element_type.3
  245.9 1.0 copy.18
  246.8 1.0 copy.19
  247.8 1.0 copy.20
  248.8 1.0 copy.21
  (1 shorter events, 0.0 us)
Async XLA Ops:
  0.6 1.6 copy-start

commit v3 on v2

--- a/solution.py
+++ b/solution.py
@@ -66,11 +66,9 @@
 
 
 def attend(
-    seq_rows, turn, finish, queries, keys, grad_out, starts, hyena, grad_queries, acc_keys, acc_hyena
+    seq_rows, turn, block_done, finish, queries, keys, grad_out, starts, hyena, grad_queries, acc_keys, acc_hyena
 ):
     scale = HEAD_DIM ** (-0.5)
-    acc_keys[...] = jnp.zeros_like(acc_keys)
-    acc_hyena[...] = jnp.zeros_like(acc_hyena)
     sequences = queries.shape[0] // seq_rows
 
     def query_block(base, q_first, k_first, width):
@@ -104,10 +102,12 @@
         base = b * seq_rows
         for n in range(short):
             query_block(base, n * QUERY_ROWS, 0, (n + 1) * QUERY_ROWS)
+            block_done(base + n * QUERY_ROWS)
 
         @pl.loop(short, seq_rows // QUERY_ROWS)
         def _(n):
             query_block(base, n * QUERY_ROWS, n * QUERY_ROWS - LONGEST_DOC, full)
+            block_done(base + n * QUERY_ROWS)
 
         finish(b)
 
@@ -129,13 +129,31 @@
         given[pl.ds(n, LANES, stride=blocks), :] = grad_mixed.T
 
 
-def mix_backward(seq_blocks, back_taps, taken, given, turned, grad_values, by_channel):
+def mix_backward(
+    seq_blocks, filter_done, back_taps, taken, given, turned, grad_values, by_channel
+):
     blocks = given.shape[0] // LANES
     row = lax.broadcasted_iota(jnp.int32, (LANES, LANES), 0)
     col = lax.broadcasted_iota(jnp.int32, (LANES, LANES), 1)
     block_row = lax.broadcasted_iota(jnp.int32, (blocks, LANES), 0)
     first = lax.rem(block_row, seq_blocks) == 0
     last = lax.rem(block_row, seq_blocks) == seq_blocks - 1
+
+    def pair_channel(c, carry):
+        at = pl.ds(pl.multiple_of(c * blocks, blocks), blocks)
+        own = taken[at, :]
+        before = jnp.where(first, 0.0, pltpu.roll(own, 1, 0))
+        both = jnp.concatenate([own, before], 1).astype(bf16)
+        pairs = lax.dot_general(
+            both, given[at, :].astype(bf16), contract_first, preferred_element_type=f32
+        )
+        by_lag = jnp.where(row + col >= LANES - 1, pairs[:LANES], pairs[LANES:])
+        by_lag = pltpu.roll(by_lag, 1, 1, stride=1, stride_axis=0)
+        by_channel[pl.ds(c, 1), :] = jnp.sum(by_lag, 0, keepdims=True)
+        return carry
+
+    lax.fori_loop(0, LANES, pair_channel, 0, unroll=4)
+    filter_done()
 
     def channel(c, carry):
         at = pl.ds(pl.multiple_of(c * blocks, blocks), blocks)
@@ -147,13 +165,6 @@
         near = jnp.where(row >= col, circle, 0.0).astype(bf16)
         far = jnp.where(row < col, circle, 0.0).astype(bf16)
         turned[at, :] = jnp.dot(grads, jnp.concatenate([near, far], 0), preferred_element_type=f32)
-        own = taken[at, :]
-        before = jnp.where(first, 0.0, pltpu.roll(own, 1, 0))
-        both = jnp.concatenate([own, before], 1).astype(bf16)
-        pairs = lax.dot_general(both, grad.astype(bf16), contract_first, preferred_element_type=f32)
-        by_lag = jnp.where(row + col >= LANES - 1, pairs[:LANES], pairs[LANES:])
-        by_lag = pltpu.roll(by_lag, 1, 1, stride=1, stride_axis=0)
-        by_channel[pl.ds(c, 1), :] = jnp.sum(by_lag, 0, keepdims=True)
         return carry
 
     lax.fori_loop(0, LANES, channel, 0, unroll=4)
@@ -165,11 +176,11 @@
 
 
 def head_kernel(
-    axes, queries, keys, gate, values, grad_out, starts, taps, back_taps,
+    axes, queries, keys, gate, values, grad_out, starts, all_taps,
     to_queries, to_keys, to_gate, to_values, to_filter,
     arrived, starts_in, starts_col, taken, given, turned, mixed, hyena, acc_keys, acc_hyena,
     grad_queries, grad_keys, grad_gate, grad_values, by_channel, grad_filter,
-    in_sent, in_got, out_sent, out_got,
+    near_filter, taps_in, taps, back_taps, in_sent, in_got, out_sent, out_got, taps_got,
 ):
     tok_rows = queries.shape[0]
     per_seq = lax.axis_size("ctx")
@@ -203,6 +214,8 @@
     def rows_of(part):
         return rows_at(part * tok_rows, tok_rows)
 
+    own_taps = pltpu.make_async_copy(all_taps.at[:, lanes_of(me)], taps_in, taps_got)
+    own_taps.start()
     barrier = pltpu.get_barrier_semaphore()
     others(lambda peer: pl.semaphore_signal(
         barrier, inc=1, device_id=device(peer), device_id_type=pl.DeviceIdType.MESH
@@ -224,6 +237,14 @@
         whole = starts_in if at == 5 else arrived.at[at]
         pltpu.make_async_copy(whole, whole, in_got.at[at]).wait()
 
+    row = lax.broadcasted_iota(jnp.int32, (LANES, LANES), 0)
+    col = lax.broadcasted_iota(jnp.int32, (LANES, LANES), 1)
+    own_taps.wait()
+    taps[...] = taps_in[...].T
+    turn_back = jnp.where(lax.rem(row + col, LANES) == 0, 1.0, 0.0).astype(bf16)
+    back_taps[...] = jnp.dot(
+        taps[...].astype(bf16), turn_back, preferred_element_type=f32
+    )
     v, gates, k, q, g = (arrived.at[at] for at in range(5))
     mix_forward(seq_blocks, wait_for, v, gates, taps, taken, turned, mixed, hyena)
     wait_for(5)
@@ -234,10 +255,12 @@
         turned_line = jnp.broadcast_to(line, (LANES, LANES)).T
         starts_col[rows_at(part * LANES, LANES), :] = turned_line[:, :1].astype(jnp.int32)
 
+    acc_keys[...] = jnp.zeros_like(acc_keys)
+    acc_hyena[...] = jnp.zeros_like(acc_hyena)
     for at in (2, 3, 4):
         wait_for(at)
 
-    results = ((grad_queries, to_queries), (grad_keys, to_keys), (grad_gate, to_gate))
+    results = ((1, grad_keys, to_keys), (2, grad_gate, to_gate))
 
     def give(at, source, target, peer):
         @pl.when(peer != me)
@@ -248,32 +271,68 @@
         def _():
             pltpu.make_async_copy(source, target, out_got.at[at]).start()
 
+    def block_done(first_row):
+        for part in range(QUERY_ROWS // tok_rows):
+            peer = lax.div(first_row, tok_rows) + part
+            give(0, grad_queries.at[rows_of(peer)], to_queries.at[:, lanes_of(me)], peer)
+
     def finish(b):
         finish_sequence(
             b, seq_blocks, gates, mixed, acc_keys, acc_hyena, grad_keys, grad_gate, given
         )
-        for at, (source, target) in enumerate(results):
+        for at, source, target in results:
             @pl.loop(0, per_seq)
             def _(step):
                 peer = b * per_seq + lax.rem(step + lax.axis_index("ctx"), per_seq)
                 give(at, source.at[rows_of(peer)], target.at[:, lanes_of(me)], peer)
 
     attend(
-        seq_rows, turn, finish, q, k, g, starts_col, hyena, grad_queries, acc_keys, acc_hyena
+        seq_rows, turn, block_done, finish, q, k, g, starts_col, hyena, grad_queries, acc_keys, acc_hyena
     )
-    mix_backward(seq_blocks, back_taps, taken, given, turned, grad_values, by_channel)
-    grad_filter[...] = by_channel[...].T.astype(bf16)
+    mine = lax.axis_index("ctx")
+
+    def seq_device(step):
+        peer = lax.rem(mine + step, per_seq)
+        return turn * per_seq + peer if "dp" in axes else peer
+
+    def filter_done():
+        grad_filter[...] = by_channel[...].T.astype(bf16)
+        landing = near_filter.at[:, lanes_of(mine)]
+
+        @pl.loop(1, per_seq)
+        def _(step):
+            send(grad_filter, landing, out_sent.at[4], out_got.at[4], seq_device(step))
+
+        pltpu.make_async_copy(grad_filter, landing, out_got.at[4]).start()
+
+    mix_backward(
+        seq_blocks, filter_done, back_taps, taken, given, turned, grad_values, by_channel
+    )
     own_lanes = lanes_of(me)
-    others(lambda peer: send(
-        grad_values.at[rows_of(peer)], to_values.at[:, own_lanes], out_sent.at[3], out_got.at[3], peer
-    ))
+
+    def give_values(begin, end):
+        @pl.loop(begin, end)
+        def _(step):
+            peer = lax.rem(me + step, parts)
+            send(
+                grad_values.at[rows_of(peer)], to_values.at[:, own_lanes],
+                out_sent.at[3], out_got.at[3], peer,
+            )
+
+    give_values(1, parts // 2)
     pltpu.make_async_copy(
         grad_values.at[rows_of(me)], to_values.at[:, own_lanes], out_got.at[3]
     ).start()
-    others(lambda peer: send(
-        grad_filter, to_filter.at[:, own_lanes], out_sent.at[4], out_got.at[4], peer
-    ))
-    pltpu.make_async_copy(grad_filter, to_filter.at[:, own_lanes], out_got.at[4]).start()
+    pltpu.make_async_copy(near_filter, near_filter, out_got.at[4]).wait()
+    span = per_seq * LANES
+    landing = to_filter.at[:, pl.ds(pl.multiple_of(turn * span, LANES), span)]
+    for step in range(1, parts // per_seq):
+        send(
+            near_filter, landing, out_sent.at[5], out_got.at[5],
+            lax.rem(me + step * per_seq, parts),
+        )
+    pltpu.make_async_copy(near_filter, landing, out_got.at[5]).start()
+    give_values(parts // 2, parts)
 
     remote = pl.ds(0, (parts - 1) * LANES)
     for at in range(5):
@@ -281,17 +340,21 @@
         pltpu.make_async_copy(sent, sent, in_sent.at[at]).wait()
     sent = starts_in.at[pl.ds(0, parts - 1)]
     pltpu.make_async_copy(sent, sent, in_sent.at[5]).wait()
-    for at, target in enumerate((to_queries, to_keys, to_gate, to_values, to_filter)):
+    for at, target in enumerate((to_queries, to_keys, to_gate, to_values)):
         pltpu.make_async_copy(target, target, out_got.at[at]).wait()
         sent = target.at[:, remote]
         pltpu.make_async_copy(sent, sent, out_sent.at[at]).wait()
+    sent = near_filter.at[:, pl.ds(0, span - LANES)]
+    pltpu.make_async_copy(sent, sent, out_sent.at[4]).wait()
+    pltpu.make_async_copy(to_filter, to_filter, out_got.at[5]).wait()
+    if parts > per_seq:
+        sent = to_filter.at[:, pl.ds(0, parts * LANES - span)]
+        pltpu.make_async_copy(sent, sent, out_sent.at[5]).wait()
 
 
 def on_device(queries, keys, gate, values, grad_out, doc_start, filter_taps, *, axes, parts):
     tok_rows, channels = queries.shape[1:]
     rows = parts * tok_rows
-    own_taps = lax.dynamic_slice_in_dim(filter_taps, lax.axis_index(axes) * LANES, LANES, 1).T
-    back_taps = jnp.roll(own_taps[:, ::-1], 1, 1)
     starts = jnp.broadcast_to(doc_start, (8, tok_rows))
     vmem = pl.BlockSpec(memory_space=pltpu.VMEM)
     anywhere = pl.BlockSpec(memory_space=pl.ANY)
@@ -301,7 +364,7 @@
         functools.partial(head_kernel, axes),
         out_shape=[jax.ShapeDtypeStruct((tok_rows, channels), bf16)] * 4
         + [jax.ShapeDtypeStruct(filter_taps.shape, bf16)],
-        in_specs=[anywhere] * 5 + [vmem] * 3,
+        in_specs=[anywhere] * 5 + [vmem, anywhere],
         out_specs=[anywhere] * 5,
         scratch_shapes=[
             pltpu.VMEM((5, rows, LANES), bf16),
@@ -311,15 +374,20 @@
             narrow, narrow, narrow, narrow,
             pltpu.VMEM((LANES, LANES), f32),
             pltpu.VMEM((LANES, LANES), bf16),
+            pltpu.VMEM((LANES, lax.axis_size("ctx") * LANES), bf16),
+            pltpu.VMEM((LANES, LANES), f32),
+            pltpu.VMEM((LANES, LANES), f32),
+            pltpu.VMEM((LANES, LANES), f32),
             pltpu.SemaphoreType.DMA((6,)),
             pltpu.SemaphoreType.DMA((6,)),
-            pltpu.SemaphoreType.DMA((5,)),
-            pltpu.SemaphoreType.DMA((5,)),
+            pltpu.SemaphoreType.DMA((6,)),
+            pltpu.SemaphoreType.DMA((6,)),
+            pltpu.SemaphoreType.DMA,
         ],
         compiler_params=pltpu.CompilerParams(
             collective_id=0, has_side_effects=True, vmem_limit_bytes=48 * 2**20
         ),
-    )(queries[0], keys[0], gate[0], values[0], grad_out[0], starts, own_taps, back_taps)
+    )(queries[0], keys[0], gate[0], values[0], grad_out[0], starts, filter_taps)
     grad_filter = grad_filter.astype(f32)
     if "dp" not in axes:
         grad_filter = lax.psum(grad_filter, "dp")

time: 250 us -> 232 us (0.928); the launches traced: 250 us -> 228 us
  Pallas kernels: 242 us -> 221 us
    pallas_call x1, Pallas kernels: 242 us -> 221 us  [on_device(): pl.pallas_call(functools.partial(head_kernel, axes), out_shape=[jax.Shape...]
where the time goes in v3:
time: 232 us; the launch traced here: 228 us
  Pallas kernels  221 us (95%)
  local copies, waits for them, and re-layouts  4.54 us (2%)
    pallas_call x1, Pallas kernels, on_device(): pl.pallas_call(functools.partial(head_kernel, axes), out_shape=[jax.Shape...  221 us

profile of v3, /device:TPU:0, one launch (start us, length us, event | category | flops | bytes accessed | tf_op | source)
XLA Modules:
  0.0 228.0 jit_solution(12465430694700859090)
XLA Ops:
  0.6 0.7 broadcast_in_dim.20.starts
  1.3 221.3 %shard_map.110 = (bf16[128,4096]{1,0:T(8,128)(2,1)S(1)}, bf16[128,4096]{1,0:T(8,128)(2,1)S(1)}, bf16[128,4096]{1,0:T(8,128)(2,1)S(1)}, bf16[128,4096]{1,0:T(8,128)(2,1)S(1)}, bf16[128,4096]{1,0:T(8,128)(2,1)S(1)}) custom-call(bf16[128,4096]{1,0:T(8,128)(2,1)} %bitcast.14, bf16[128,4096]{1,0:T(8,128)(2,1)} %bitcast.15, bf16[128,4096]{1,0:T(8,128)(2,1)} %bitcast.16, ...), custom_call_target="tpu_custom_call" | custom-call | tf_op jit(solution)/shard_map/pallas_call | solution.py:363
  222.6 1.5 convert_element_type.3
  224.1 1.0 copy.16
  225.1 1.0 copy.17
  226.0 1.0 copy.18
  227.0 1.0 copy.19
